TPU v7x, 256 devices: a whole 4x4x8 slice. The times are simulated.
256 devices in a mesh: dp: 32 (over z, y), tensor: 8 (over x, core).
Axes of the slice: x: 4, y: 4, z: 8, core: 2. Of those that a mesh axis runs over, the one named last changes fastest.
Arguments:
- queries: bfloat16 [24576, 4096], P('dp', 'tensor'), may hold values from -8 to 8
- step_kv: bfloat16 [2, 24576, 1024], P(None, 'dp', 'tensor'), may hold values from -6 to 6
- tile_kv: bfloat16 [2, 262144, 1024], P(None, 'dp', 'tensor'), may hold values from -6 to 6
- tile_slot: int32 [1024], replicated, may hold values from 0 to 127, as said below
- step_lengths: int32 [128, 8], replicated, may hold values from 1 to 24, 120 in all within a row
- parents: int32 [128, 8], replicated, may hold values from -1 to 6, as said below
- out_weight: bfloat16 [4096, 8192], P('dp', 'tensor'), may hold values from -0.09375 to 0.09375
Outputs:
- mixed_out: bfloat16 [24576, 8192], P('dp', 'tensor')
Inputs may be any that keep to these rules, and one draw needn't show every extreme that they name: `tile_slot`: tile t is encoded on index t // 32 of dp; problem p's steps lie on index p // 4 of dp. Each problem owns 1 to 12 tiles and on every index one of its problems owns exactly 12; the problems of one index own exactly 32 tiles together; the tiles of one encoding index that belong to the problems of one index number at most 2, and exactly 2 for some. parents[p, 0] = -1; for s >= 1, parents[p, s] is a step before s. `step_lengths`: row p holds the token counts of problem p's 8 steps.
All inputs are finite; a program needn't handle non-finite values.
Results may differ from a plain program's by a relative error of at most 0.0052.
Values may be sent and summed in bfloat16 or wider, within the bound.
A program may use at most 128 MiB of HBM per device.

v0:
```python
import math

import jax
import jax.numpy as jnp
from jax import lax
from jax.sharding import PartitionSpec as P

HD = 128
TILE = 256
TILE_MAX = 12
STEPS = 8
STEP_LEN = 24


def ancestry(parents_row):
    parent_links = (parents_row[:, None] == jnp.arange(STEPS, dtype=jnp.int32)[None, :]).astype(
        jnp.int32
    )
    reached = jnp.eye(STEPS, dtype=jnp.int32)
    frontier = reached
    for depth_step in range(STEPS - 1):
        frontier = jnp.minimum(jnp.dot(frontier, parent_links), 1)
        reached = jnp.maximum(reached, frontier)
    return reached > 0


def visibility(lengths_row, parents_row):
    reached = ancestry(parents_row)
    token_index = jnp.arange(STEPS * STEP_LEN, dtype=jnp.int32)
    step_of = token_index // STEP_LEN
    position = token_index % STEP_LEN
    reached_full = jnp.repeat(jnp.repeat(reached, STEP_LEN, axis=0), STEP_LEN, axis=1)
    length_of = jnp.repeat(lengths_row, STEP_LEN)
    key_live = position < length_of
    same_step = step_of[:, None] == step_of[None, :]
    visible = (
        reached_full
        & key_live[None, :]
        & (jnp.logical_not(same_step) | (position[None, :] <= position[:, None]))
    )
    return (visible, key_live)


def attend(query_block, key_rows, value_rows, key_mask, live_rows):
    scores = jnp.einsum(
        "qkgd,nkd->kgqn", query_block, key_rows, preferred_element_type=jnp.float32
    ) / math.sqrt(HD)
    scores = jnp.where(key_mask[None, None], scores, -jnp.inf)
    row_max = jnp.max(scores, axis=-1, keepdims=True)
    exponent = jnp.exp(scores - row_max)
    totals = jnp.sum(exponent, axis=-1, keepdims=True)
    weights = exponent.astype(jnp.bfloat16)
    result = jnp.einsum("kgqn,nkd->qkgd", weights, value_rows, preferred_element_type=jnp.float32)
    result = result / jnp.transpose(totals, (2, 0, 1, 3))
    result = jnp.where(live_rows[:, None, None, None], result, 0.0)
    return result.astype(jnp.bfloat16)


def per_device(queries, step_kv, tile_kv, tile_slot, step_lengths, parents, out_weight):
    senders = lax.axis_size("dp")
    own_index = lax.axis_index("dp")
    step_span = STEPS * STEP_LEN
    problems = queries.shape[0] // step_span
    kv_width = step_kv.shape[2]
    kv_heads = kv_width // HD
    group_size = queries.shape[1] // kv_width
    tile_count = tile_kv.shape[1] // TILE
    capacity = max(2, 2 * tile_count // senders)
    peer_ids = jnp.arange(senders, dtype=jnp.int32)
    owners = tile_slot.reshape(senders, tile_count)
    destination = owners // problems
    outgoing_dest = lax.dynamic_index_in_dim(destination, own_index, 0, keepdims=False)
    matches = (outgoing_dest[:, None] == peer_ids[None, :]).astype(jnp.int32)
    position = jnp.sum((jnp.cumsum(matches, axis=0) - 1) * matches, axis=1)
    location = outgoing_dest * capacity + position
    tile_blocks = tile_kv.reshape(2, tile_count, TILE, kv_width)
    outgoing = (
        jnp.zeros((2, senders * capacity, TILE, kv_width), jnp.bfloat16)
        .at[:, location]
        .set(tile_blocks)
    )
    incoming = lax.all_to_all(
        outgoing.reshape(2, senders, capacity, TILE, kv_width),
        "dp",
        split_axis=1,
        concat_axis=1,
        tiled=True,
    )
    incoming = incoming.reshape(2, senders * capacity, TILE, kv_width)
    arriving = destination == own_index
    arrival = jnp.cumsum(arriving.astype(jnp.int32), axis=1) - 1
    slot_flat = (peer_ids[:, None] * capacity + arrival).reshape(-1)
    local_owner = (owners - own_index * problems).reshape(-1)
    arriving_flat = arriving.reshape(-1)
    belongs = arriving_flat[None, :] & (
        local_owner[None, :] == jnp.arange(problems, dtype=jnp.int32)[:, None]
    )
    ranking = jnp.cumsum(belongs.astype(jnp.int32), axis=1) - 1
    selected = belongs[:, None, :] & (
        ranking[:, None, :] == jnp.arange(TILE_MAX, dtype=jnp.int32)[None, :, None]
    )
    lookup = jnp.sum(jnp.where(selected, slot_flat[None, None, :], 0), axis=2)
    tile_live = jnp.any(selected, axis=2)
    chosen = jnp.take(incoming, lookup.reshape(-1), axis=1).reshape(
        2, problems, TILE_MAX * TILE, kv_heads, HD
    )
    lengths_here = lax.dynamic_slice_in_dim(step_lengths, own_index * problems, problems, 0)
    parents_here = lax.dynamic_slice_in_dim(parents, own_index * problems, problems, 0)
    steps_here = step_kv.reshape(2, problems, step_span, kv_heads, HD)
    query_here = queries.reshape(problems, step_span, kv_heads, group_size, HD)

    def per_problem(inputs):
        (
            query_block,
            tile_keys,
            tile_values,
            step_keys,
            step_values,
            lengths_row,
            parents_row,
            live_tiles,
        ) = inputs
        key_rows = jnp.concatenate([tile_keys, step_keys], axis=0)
        value_rows = jnp.concatenate([tile_values, step_values], axis=0)
        visible, live_rows = visibility(lengths_row, parents_row)
        tile_seen = jnp.broadcast_to(
            jnp.repeat(live_tiles, TILE)[None, :], (step_span, TILE_MAX * TILE)
        )
        key_mask = jnp.concatenate([tile_seen, visible], axis=1)
        return attend(query_block, key_rows, value_rows, key_mask, live_rows).reshape(
            step_span, group_size * kv_width
        )

    head_out = lax.map(
        per_problem,
        (
            query_here,
            chosen[0],
            chosen[1],
            steps_here[0],
            steps_here[1],
            lengths_here,
            parents_here,
            tile_live,
        ),
    )
    head_out = head_out.reshape(problems * step_span, group_size * kv_width)
    full_rows = lax.all_gather(out_weight, "dp", axis=0, tiled=True)
    mixed_out = jnp.dot(
        lax.all_gather(head_out, "tensor", axis=1, tiled=True),
        full_rows,
        preferred_element_type=jnp.float32,
    )
    return mixed_out.astype(jnp.bfloat16)


def solution(mesh):
    return jax.shard_map(
        per_device,
        mesh=mesh,
        in_specs=(
            P("dp", "tensor"),
            P(None, "dp", "tensor"),
            P(None, "dp", "tensor"),
            P(),
            P(),
            P(),
            P("dp", "tensor"),
        ),
        out_specs=P("dp", "tensor"),
        check_vma=False,
    )
```

profile of v0, /device:TPU:6, one launch (start us, length us, event | category | flops | bytes accessed | tf_op | source)
XLA Modules:
  0.0 411.8 jit_solution(17376992196739531115)
XLA Ops:
  7.7 4.7 %copy.54 = bf16[2,32,256,128]{3,2,0,1:T(8,128)(2,1)} copy(bf16[2,32,256,128]{3,2,1,0:T(8,128)(2,1)} %bitcast.153) | data formatting | bytes 8388608 | tf_op jit(solution)/shard_map/reshape | solution.py:76
  12.3 5.3 %broadcast_in_dim.136 = bf16[2,64,256,128]{3,2,1,0:T(8,128)(2,1)} broadcast(bf16[]{:T(256)} %constant.127.clone.1), dimensions={} | broadcast | bytes 8388610 | tf_op jit(solution)/shard_map/broadcast_in_dim | solution.py:78
  17.6 11.1 %scatter_fusion = bf16[2,64,256,128]{3,2,1,0:T(8,128)(2,1)} fusion(bf16[2,64,256,128]{3,2,1,0:T(8,128)(2,1)} %broadcast_in_dim.136, s32[32]{0:T(128)S(1)} %fusion.50, bf16[32,2,256,128]{3,2,1,0:T(8,128)(2,1)} %bitcast.150), kind=kCustom, calls=%fused_computation.1 | custom fusion | bytes 12583040 | tf_op jit(solution)/shard_map/scatter | solution.py:80
  28.7 7.7 %copy.36 = bf16[2,32,2,256,128]{4,3,2,0,1:T(8,128)(2,1)} copy(bf16[2,32,2,256,128]{4,3,2,1,0:T(8,128)(2,1)} %bitcast.148) | data formatting | bytes 16777216 | tf_op jit(solution)/shard_map/reshape | solution.py:83
  36.5 11.7 %all-to-all-start = ((bf16[2,32,2,256,128]{4,3,2,0,1:T(8,128)(2,1)}), bf16[2,32,2,256,128]{4,3,2,0,1:T(8,128)(2,1)}, u32[]{:S(2)}, u32[]{:S(2)}) async-start(bf16[2,32,2,256,128]{4,3,2,0,1:T(8,128)(2,1)} %copy.36), calls=%async_computation | async-start | bytes 16777216 | tf_op jit(solution)/shard_map/all_to_all | solution.py:82
  49.3 1.1 reduce-window.6
  52.5 1.1 reshape.356
  54.5 225.9 %all-to-all-done = bf16[2,32,2,256,128]{4,3,2,0,1:T(8,128)(2,1)} async-done(((bf16[2,32,2,256,128]{4,3,2,0,1:T(8,128)(2,1)}), bf16[2,32,2,256,128]{4,3,2,0,1:T(8,128)(2,1)}, u32[]{:S(2)}, u32[]{:S(2)}) %all-to-all-start) | async-done | bytes 8388640 | tf_op jit(solution)/shard_map/all_to_all | solution.py:82
  280.4 7.7 %copy.37 = bf16[2,32,2,256,128]{4,3,2,1,0:T(8,128)(2,1)} copy(bf16[2,32,2,256,128]{4,3,2,0,1:T(8,128)(2,1)} %all-to-all-done) | data formatting | bytes 16777216 | tf_op jit(solution)/shard_map/all_to_all | solution.py:82
  288.1 8.4 %gather_fusion = bf16[48,2,256,128]{3,2,1,0:T(8,128)(2,1)} fusion(bf16[2,64,256,128]{3,2,1,0:T(8,128)(2,1)} %bitcast.149, s32[1024]{0:T(1024)S(1)} %pad_clamp_fusion), kind=kCustom, calls=%fused_computation | custom fusion | bytes 12583104 | tf_op jit(solution)/shard_map/jit(_take)/gather | solution.py:104
  296.5 3.4 select_bitcast_fusion
  300.0 2.2 fusion.54
  302.2 46.6 %while.12 = (s32[]{:T(128)}, bf16[4,192,512]{2,1,0:T(8,128)(2,1)}, s32[4,8]{1,0:T(4,128)S(1)}, bf16[4,3072,1,128]{3,1,2,0:T(8,128)(2,1)}, bf16[4,192,1,128]{3,1,...) while((s32[]{:T(128)}, bf16[4,192,512]{2,1,0:T(8,128)(2,1)}, ...), condition=%wide.region_11.12_spmd, body=%wide.region_8.11_spmd.sunk | while | flops 1305500288 | bytes 38514156 | solution.py:134
  304.6 1.2 dynamic-slice_bitcast_fusion.7
  306.7 1.0 constant_dynamic-slice_fusion.8
  307.7 2.1 fusion.93
  309.8 1.5 fusion.94
  311.3 1.6 fusion.95
  316.2 1.2 dynamic-slice_bitcast_fusion.7
  319.3 2.1 fusion.93
  321.5 1.5 fusion.94
  322.9 1.6 fusion.95
  327.9 1.2 dynamic-slice_bitcast_fusion.7
  331.0 2.1 fusion.93
  333.1 1.5 fusion.94
  334.6 1.6 fusion.95
  339.5 1.2 dynamic-slice_bitcast_fusion.7
  342.6 2.1 fusion.93
  344.8 1.5 fusion.94
  346.3 1.6 fusion.95
  348.8 44.1 %all-gather.3.cloned.1.call-done = bf16[768,4096]{1,0:T(8,128)(2,1)} async-done(((bf16[768,512]{1,0:T(8,128)(2,1)}), bf16[768,4096]{1,0:T(8,128)(2,1)}) %all-gather.3.cloned.1.call-update) | async-done | bytes 6291472 | tf_op jit(solution)/shard_map/all_gather | solution.py:150
  392.9 12.1 %convolution_convert_fusion = bf16[768,1024]{1,0:T(8,128)(2,1)} fusion(bf16[768,4096]{1,0:T(8,128)(2,1)} %all-gather.3.cloned.1.call-done, bf16[4096,1024]{1,0:T(8,128)(2,1)} %all-gather.5.cloned.1.call-done), kind=kOutput, calls=%fused_computation.64 | convolution fusion | flops 6443237376 | bytes 16252928 | tf_op jit(solution)/shard_map/dot_general | solution.py:149
  (158 shorter events, 24.6 us)
Async XLA Ops:
  36.5 12.7 %copy-start.2 = (s32[1024]{0:T(1024)S(1)}, s32[1024]{0:T(1024)}, u32[]{:S(2)}) copy-start(s32[1024]{0:T(1024)} %param.12) | copy-start | bytes 12292
  36.5 15.8 %copy-start.3 = (s32[128,8]{0,1:T(8,128)S(1)}, s32[128,8]{0,1:T(8,128)}, u32[]{:S(2)}) copy-start(s32[128,8]{0,1:T(8,128)} %param.14) | copy-start | bytes 12292
  36.5 15.8 %copy-start.4 = (s32[128,8]{0,1:T(8,128)S(1)}, s32[128,8]{0,1:T(8,128)}, u32[]{:S(2)}) copy-start(s32[128,8]{0,1:T(8,128)} %param.13) | copy-start | bytes 12292
  36.5 16.1 %copy-start = (bf16[768,512]{1,0:T(8,128)(2,1)S(1)}, bf16[768,512]{1,0:T(8,128)(2,1)}, u32[]{:S(2)}) copy-start(bf16[768,512]{1,0:T(8,128)(2,1)} %param.9) | copy-start | bytes 2359300
  36.5 17.2 %copy-start.1 = (bf16[2,768,128]{2,1,0:T(8,128)(2,1)S(1)}, bf16[2,768,128]{2,1,0:T(8,128)(2,1)}, u32[]{:S(2)}) copy-start(bf16[2,768,128]{2,1,0:T(8,128)(2,1)} %param.10) | copy-start | bytes 1179652
  36.5 243.9 %all-to-all-start = ((bf16[2,32,2,256,128]{4,3,2,0,1:T(8,128)(2,1)}), bf16[2,32,2,256,128]{4,3,2,0,1:T(8,128)(2,1)}, u32[]{:S(2)}, u32[]{:S(2)}) async-start(bf16[2,32,2,256,128]{4,3,2,0,1:T(8,128)(2,1)} %copy.36), calls=%async_computation | async-start | bytes 16777216 | tf_op jit(solution)/shard_map/all_to_all | solution.py:82
  48.2 300.6 %all-gather.5.cloned.1.call-start = ((), (), s32[]{:S(2)}) async-start(), calls=%async_computation.2 | async-start | bytes 8650752 | tf_op jit(solution)/shard_map/all_gather | solution.py:148
  49.0 344.0 %all-gather.3.cloned.1.call-start = ((), (), s32[]{:S(2)}) async-start(), calls=%async_computation.1 | async-start | bytes 7077888 | tf_op jit(solution)/shard_map/all_gather | solution.py:150
Sparse Core Ops, SparseCore 0:
  51.7 222.0 all-gather.4
  348.9 43.9 all-gather.2
where the time goes:
time: 416 us; the launch traced here: 412 us
  waiting for transfers between devices  271 us (65%)
  local copies, waits for them, and re-layouts  69.4 us (17%)
  matrix products  32.3 us (8%)
  between operations  13.6 us (3%)
  other arithmetic  13.5 us (3%)
  starting transfers between devices  12 us (3%)
    all_to_all x1, waiting for transfers between devices, per_device(): lax.all_to_all(outgoing.reshape(2, senders, capacity, TILE, kv_width), 'd...  226 us
    all_gather x1, waiting for transfers between devices, per_device(): lax.all_gather(head_out, 'tensor', axis=1, tiled=True)  44.1 us
    dot_general x1, matrix products, per_device(): jnp.dot(lax.all_gather(head_out, 'tensor', axis=1, tiled=True), full_rows...  12.1 us
    all_to_all x1, starting transfers between devices, per_device(): lax.all_to_all(outgoing.reshape(2, senders, capacity, TILE, kv_width), 'd...  11.7 us
    scatter x1, local copies, waits for them, and re-layouts, per_device(): outgoing = jnp.zeros((2, senders * capacity, TILE, kv_width), jnp.bfloat1...  11.1 us
    dot_general x4, matrix products, attend(): jnp.einsum('qkgd,nkd->kgqn', query_block, key_rows, preferred_element_typ...  8.51 us
    gather x1, local copies, waits for them, and re-layouts, per_device(): jnp.take(incoming, lookup.reshape(-1), axis=1)  8.4 us
    squeeze x16, local copies, waits for them, and re-layouts, per_device(): lax.map(per_problem, (query_here, chosen[0], chosen[1], steps_here[0], st...  8.39 us
  transfers between devices with their start and end apart: 3, of which 2 were waited for; matrix products, arithmetic and copies ran while one was open for 18% of the time, Pallas kernels for 0%

commit v1 on v0

v1 whole, which is shorter than its diff:
```python
import functools
import math

import jax
import jax.numpy as jnp
from jax import lax
from jax.experimental import pallas as pl
from jax.experimental.pallas import tpu as pltpu
from jax.sharding import PartitionSpec as P

HD = 128
TILE = 256
STEPS = 8
STEP_LEN = 24
SPAN = STEPS * STEP_LEN
PROBLEMS = 4
GROUP = 4
LIVE = 128
LANES = GROUP * LIVE
Z = 8
Y = 4
X = 4
LOW = -1e30
SCALE = math.log2(math.e) / math.sqrt(HD)
MESH = pl.DeviceIdType.MESH
ORDER = (4, 3, 5, 2, 6, 1, 7, 0)
MIB = 1 << 20

META_ORDER = 0
META_OWNER = 64
META_SAME = 128
META_LAST = 192


def dot(a, b, dims=((1,), (0,))):
    return lax.dot_general(a, b, (dims, ((), ())), preferred_element_type=jnp.float32)


def prep_kernel(
    slot_ref, length_ref, parent_ref, query_ref, tile_ref,
    send_ref, qt_ref, mask_ref, expand_ref, meta_ref,
    count, count_in, owner_of, sems,
):
    dp = lax.axis_index("dp")
    z, y = dp // Y, dp % Y

    def clear(i, _):
        count[i] = 0
        count_in[i] = 0
        return 0

    lax.fori_loop(0, 32, clear, 0)

    def clear_slots(i, _):
        owner_of[i] = -1
        meta_ref[META_ORDER + i] = 0
        meta_ref[META_OWNER + i] = 0
        meta_ref[META_SAME + i] = 0
        meta_ref[META_LAST + i] = 0
        return 0

    lax.fori_loop(0, 64, clear_slots, 0)

    def place(t, _):
        d = slot_ref[dp * 32 + t] >> 2
        rz = ((d >> 2) - z) & 7
        r = ((d & 3) - y) & 3
        j = count[r * 8 + rz]
        count[r * 8 + rz] = j + 1
        pltpu.make_async_copy(
            tile_ref.at[:, pl.ds(pl.multiple_of(t * TILE, TILE), TILE), :],
            send_ref.at[r, rz, j],
            sems.at[t],
        ).start()
        return 0

    lax.fori_loop(0, 32, place, 0)

    def arrive(q, _):
        s = slot_ref[z * 128 + q]
        d = s >> 2

        @pl.when((d & 3) == y)
        def _():
            rz = ((d >> 2) - z) & 7
            r = (y - (q >> 5)) & 3
            j = count_in[r * 8 + rz]
            count_in[r * 8 + rz] = j + 1
            owner_of[rz * 8 + r * 2 + j] = s & 3

        return 0

    lax.fori_loop(0, 128, arrive, 0)

    def arrange(i, n):
        rz, p = i // 4, i % 4
        n = jnp.where(p == 0, 0, n)

        def scan(s, carry):
            n, seen = carry
            match = owner_of[rz * 8 + s] == p

            @pl.when(match)
            def _():
                meta_ref[META_ORDER + rz * 8 + n] = s
                meta_ref[META_OWNER + rz * 8 + n] = p
                meta_ref[META_SAME + rz * 8 + n] = seen
                meta_ref[META_LAST + rz * 4 + p] = n + 1

            hit = match.astype(jnp.int32)
            return n + hit, jnp.maximum(seen, hit)

        n, _ = lax.fori_loop(0, 8, scan, (n, 0))
        return n

    lax.fori_loop(0, 32, arrange, 0)

    row = lax.broadcasted_iota(jnp.int32, (SPAN, LIVE), 0)
    lane = lax.broadcasted_iota(jnp.int32, (SPAN, LIVE), 1)
    step_of = row // STEP_LEN
    position = row - step_of * STEP_LEN
    for p in range(PROBLEMS):
        problem = dp * PROBLEMS + p
        lengths = [length_ref[problem, s] for s in range(STEPS)]
        links = [parent_ref[problem, s] for s in range(STEPS)]
        starts, lines = [], []
        total = jnp.int32(0)
        for s in range(STEPS):
            starts.append(total)
            total = total + lengths[s]
            line = jnp.int32(1 << s)
            for b in range(s):
                line = line | jnp.where(links[s] == b, lines[b], 0)
            lines.append(line)
        row_start, row_length = jnp.zeros_like(row), jnp.zeros_like(row)
        row_bit = jnp.zeros_like(row)
        lane_step, lane_start, lane_line = jnp.zeros_like(row), jnp.zeros_like(row), jnp.zeros_like(row)
        for s in range(STEPS):
            here = step_of == s
            row_start = jnp.where(here, starts[s], row_start)
            row_length = jnp.where(here, lengths[s], row_length)
            row_bit = jnp.where(here, 1 << s, row_bit)
            passed = lane >= starts[s]
            lane_step = jnp.where(passed, s, lane_step)
            lane_start = jnp.where(passed, starts[s], lane_start)
            lane_line = jnp.where(passed, lines[s], lane_line)
        live = position < row_length
        picked = (lane == row_start + position) & live
        expand = jnp.where(picked, 1.0, 0.0).astype(jnp.bfloat16)
        expand_ref[p] = expand
        visible = (
            ((lane_line & row_bit) != 0)
            & live
            & ((step_of != lane_step) | (position <= lane - lane_start))
        )
        mask_ref[p] = jnp.where(visible, 1.0, 0.0)
        for h in range(GROUP):
            block = query_ref[p * SPAN : (p + 1) * SPAN, h * HD : (h + 1) * HD]
            qt_ref[p, :, h * LIVE : (h + 1) * LIVE] = dot(block, expand, ((0,), (0,))).astype(
                jnp.bfloat16
            )

    def settle(t, _):
        pltpu.make_async_copy(
            tile_ref.at[:, pl.ds(0, TILE), :], send_ref.at[0, 0, 0], sems.at[t]
        ).wait()
        return 0

    lax.fori_loop(0, 32, settle, 0)


def plane_kernel(
    meta_ref, send_ref, qt_ref, step_ref, mask_ref,
    out_ref,
    *scratch,
):
    tiles = scratch[0:8]
    qs = (qt_ref,) + tuple(scratch[8:15])
    (
        relay, state_o, state_m, state_l, step_o, step_m, step_l,
        up_in, up_in_s, up_out, up_out_s, down_in, down_in_s, down_out, down_out_s,
        own_sem, y_send, y_recv, q_send, q_recv, c_send, c_recv, x_send, x_recv,
    ) = scratch[15:]
    dp, tensor = lax.axis_index("dp"), lax.axis_index("tensor")
    z, y = dp // Y, dp % Y
    x, core = tensor // 2, tensor % 2
    y_up = (z * Y + (y + 1) % Y, tensor)
    y_down = (z * Y + (y + Y - 1) % Y, tensor)
    z_up = (((z + 1) % Z) * Y + y, tensor)
    z_down = (((z + Z - 1) % Z) * Y + y, tensor)
    x_up = (dp, ((x + 1) % X) * 2 + core)
    x_down = (dp, ((x + X - 1) % X) * 2 + core)
    mate = (dp, x * 2 + 1 - core)

    barrier = pltpu.get_barrier_semaphore()
    peers = (y_up, y_down, z_up, z_down, x_up, x_down, mate)
    for peer in peers:
        pl.semaphore_signal(barrier, inc=1, device_id=peer, device_id_type=MESH)
    pl.semaphore_wait(barrier, len(peers))

    def remote(src, dst, send_sem, recv_sem, peer):
        return pltpu.make_async_remote_copy(
            src_ref=src, dst_ref=dst, send_sem=send_sem, recv_sem=recv_sem,
            device_id=peer, device_id_type=MESH,
        )

    def q_copies(hop):
        up_from, up_to = (8 - hop) % 8, 7 - hop
        up_src, up_dst = qs[up_from], qs[up_to]
        down_src, down_dst = qs[hop], qs[hop + 1]
        if hop == 3:
            up_src, up_dst = up_src.at[pl.ds(0, 2)], up_dst.at[pl.ds(0, 2)]
            down_src, down_dst = down_src.at[pl.ds(2, 2)], down_dst.at[pl.ds(2, 2)]
        return (
            remote(up_src, up_dst, q_send.at[hop, 0], q_recv.at[hop, 0], z_up),
            remote(down_src, down_dst, q_send.at[hop, 1], q_recv.at[hop, 1], z_down),
        )

    def direct(i):
        rz = ORDER[i]
        return (
            remote(send_ref.at[1, rz], tiles[rz].at[pl.ds(2, 2)], y_send.at[i, 0], y_recv.at[i, 0], y_up),
            remote(send_ref.at[3, rz], tiles[rz].at[pl.ds(6, 2)], y_send.at[i, 1], y_recv.at[i, 1], y_down),
        )

    def first_leg(i):
        rz = ORDER[i]
        return (
            remote(send_ref.at[2, rz, 0], relay.at[i, 0], y_send.at[i, 2], y_recv.at[i, 2], y_up),
            remote(send_ref.at[2, rz, 1], relay.at[i, 1], y_send.at[i, 3], y_recv.at[i, 3], y_down),
        )

    def second_leg(i):
        rz = ORDER[i]
        return (
            remote(relay.at[i, 0], tiles[rz].at[4], y_send.at[i, 4], y_recv.at[i, 4], y_up),
            remote(relay.at[i, 1], tiles[rz].at[5], y_send.at[i, 5], y_recv.at[i, 5], y_down),
        )

    def own(i):
        rz = ORDER[i]
        return pltpu.make_async_copy(send_ref.at[0, rz], tiles[rz].at[pl.ds(0, 2)], own_sem.at[i])

    def start(copies):
        for copy in copies:
            copy.start()

    def arrived(copies):
        for copy in copies:
            copy.wait_recv()

    def pass_on(i):
        arrived(first_leg(i))
        start(second_leg(i))

    start(q_copies(0))
    for i in range(4):
        start(first_leg(i))
        if i < 3:
            start(direct(i))
    for i in range(8):
        own(i).start()

    state_o[0] = jnp.zeros((HD, LANES), jnp.float32)
    state_m[0] = jnp.full((1, LANES), LOW, jnp.float32)
    state_l[0] = jnp.zeros((1, LANES), jnp.float32)

    def soften(scores, m_before):
        m = jnp.maximum(m_before, jnp.max(scores, axis=0, keepdims=True))
        expo = jnp.exp2(scores - m)
        return m, jnp.sum(expo, axis=0, keepdims=True), expo.astype(jnp.bfloat16)

    def attend_steps(p, _):
        rows = pl.ds(pl.multiple_of(p * SPAN, SPAN), SPAN)
        mask = mask_ref[p]
        mask = jnp.concatenate([mask] * GROUP, axis=1)
        scores = dot(step_ref[0, rows, :], qt_ref[p]) * SCALE
        scores = jnp.where(mask > 0.5, scores, LOW)
        m, l, weights = soften(scores, jnp.full((1, LANES), LOW, jnp.float32))
        step_o[p] = dot(step_ref[1, rows, :], weights, ((0,), (0,)))
        step_m[p] = m
        step_l[p] = l
        return 0

    def attend_tiles(rz):
        def one(s, _):
            slot = meta_ref[META_ORDER + rz * 8 + s]
            owner = meta_ref[META_OWNER + rz * 8 + s]
            same = meta_ref[META_SAME + rz * 8 + s]
            scores = dot(tiles[rz][slot, 0], qs[rz][owner]) * SCALE
            m_before = jnp.where(same > 0, state_m[s], LOW)
            m, l, weights = soften(scores, m_before)
            alpha = jnp.exp2(m_before - m)
            state_o[s + 1] = state_o[s] * alpha + dot(tiles[rz][slot, 1], weights, ((0,), (0,)))
            state_m[s + 1] = m
            state_l[s + 1] = state_l[s] * alpha + l
            return 0

        lax.fori_loop(0, 8, one, 0)

    def chain_copies(hop, out, out_s, inn, inn_s, side, peer):
        src, dst = out.at[hop], inn.at[hop]
        if hop == 0:
            half = pl.ds(2, 2) if side == 0 else pl.ds(0, 2)
            src, dst = out.at[hop, half], inn.at[hop, half]
        return (
            remote(src, dst, c_send.at[hop, side, 0], c_recv.at[hop, side, 0], peer),
            remote(out_s.at[hop], inn_s.at[hop], c_send.at[hop, side, 1], c_recv.at[hop, side, 1], peer),
        )

    def up(hop):
        return chain_copies(hop, up_out, up_out_s, up_in, up_in_s, 0, z_up)

    def down(hop):
        return chain_copies(hop, down_out, down_out_s, down_in, down_in_s, 1, z_down)

    def pass_sums(hop, rz, side):
        copies = (up, down)[side]
        out, out_s, inn, inn_s = (
            (up_out, up_out_s, up_in, up_in_s),
            (down_out, down_out_s, down_in, down_in_s),
        )[side]
        if hop > 0:
            arrived(copies(hop - 1))
        else:
            out_s[hop] = jnp.zeros((8, LANES), jnp.float32)

        def alone(p, _):
            last = meta_ref[META_LAST + rz * 4 + p]
            out[hop, p] = state_o[last].astype(jnp.bfloat16)
            out_s[hop, pl.ds(p, 1), :] = state_m[last]
            out_s[hop, pl.ds(p + 4, 1), :] = state_l[last]
            return 0

        def merged(p, _):
            last = meta_ref[META_LAST + rz * 4 + p]
            m_a, m_b = state_m[last], inn_s[hop - 1, pl.ds(p, 1), :]
            m = jnp.maximum(m_a, m_b)
            a, b = jnp.exp2(m_a - m), jnp.exp2(m_b - m)
            out[hop, p] = (state_o[last] * a + inn[hop - 1, p].astype(jnp.float32) * b).astype(
                jnp.bfloat16
            )
            out_s[hop, pl.ds(p, 1), :] = m
            out_s[hop, pl.ds(p + 4, 1), :] = (
                state_l[last] * a + inn_s[hop - 1, pl.ds(p + 4, 1), :] * b
            )
            return 0

        half = (2, 4) if side == 0 else (0, 2)
        other = (0, 2) if side == 0 else (2, 4)
        if hop == 0:
            lax.fori_loop(*half, alone, 0)
        elif hop == 1:
            lax.fori_loop(*half, merged, 0)
            lax.fori_loop(*other, alone, 0)
        else:
            lax.fori_loop(0, 4, merged, 0)
        start(copies(hop))

    for hop in range(3):
        arrived(q_copies(hop))
        start(q_copies(hop + 1))
        pass_on(hop)
    lax.fori_loop(0, PROBLEMS, attend_steps, 0)

    for i in range(8):
        rz = ORDER[i]
        arrived(direct(i))
        arrived(second_leg(i))
        own(i).wait()
        if i + 3 < 8:
            start(direct(i + 3))
            if i + 4 < 8:
                start(first_leg(i + 4))
            pass_on(i + 3)
        if i == 0:
            arrived(q_copies(3))
        attend_tiles(rz)
        if rz == 4:
            pass_sums(0, rz, 0)
            pass_sums(0, rz, 1)
        elif rz in (3, 2, 1):
            pass_sums(4 - rz, rz, 0)
        elif rz in (5, 6, 7):
            pass_sums(rz - 4, rz, 1)
    arrived(up(3))
    arrived(down(3))

    mine = tensor

    def finish(p, _):
        last = meta_ref[META_LAST + p]
        terms = (
            (state_o[last], state_m[last], state_l[last]),
            (step_o[p], step_m[p], step_l[p]),
            (up_in[3, p].astype(jnp.float32), up_in_s[3, pl.ds(p, 1), :], up_in_s[3, pl.ds(p + 4, 1), :]),
            (down_in[3, p].astype(jnp.float32), down_in_s[3, pl.ds(p, 1), :], down_in_s[3, pl.ds(p + 4, 1), :]),
        )
        m = functools.reduce(jnp.maximum, [t[1] for t in terms])
        factors = [jnp.exp2(t[1] - m) for t in terms]
        total = sum(t[2] * f for t, f in zip(terms, factors))
        result = sum(t[0] * f for t, f in zip(terms, factors)) / total
        rows = pl.ds(pl.multiple_of(p * LIVE, LIVE), LIVE)
        for h in range(GROUP):
            block = result[:, h * LIVE : (h + 1) * LIVE]
            out_ref[mine, rows, h * HD : (h + 1) * HD] = block.T.astype(jnp.bfloat16)
        return 0

    lax.fori_loop(0, PROBLEMS, finish, 0)

    ROWS = PROBLEMS * LIVE
    left = ((x + X - 1) % X) * 2 + core
    right = ((x + 1) % X) * 2 + core
    far = ((x + 2) % X) * 2 + core
    low, high = pl.ds(0, ROWS // 2), pl.ds(ROWS // 2, ROWS // 2)

    def to(k, view, peer):
        return remote(view, view, x_send.at[k], x_recv.at[k], peer)

    own_up = to(0, out_ref.at[mine], x_up)
    own_down = to(1, out_ref.at[mine], x_down)
    own_mate = to(2, out_ref.at[mine], mate)
    start((own_up, own_down, own_mate))
    from_left = to(0, out_ref.at[left], x_up)
    from_right = to(1, out_ref.at[right], x_down)
    from_left.wait_recv()
    on_up = to(3, out_ref.at[left, low], x_up)
    left_mate = to(4, out_ref.at[left], mate)
    start((on_up, left_mate))
    from_right.wait_recv()
    on_down = to(5, out_ref.at[right, high], x_down)
    right_mate = to(6, out_ref.at[right], mate)
    start((on_down, right_mate))
    to(3, out_ref.at[far, low], x_up).wait_recv()
    to(5, out_ref.at[far, high], x_down).wait_recv()
    far_mate = to(7, out_ref.at[far], mate)
    far_mate.start()
    to(2, out_ref.at[x * 2 + 1 - core], mate).wait_recv()
    to(4, out_ref.at[((x + X - 1) % X) * 2 + 1 - core], mate).wait_recv()
    to(6, out_ref.at[((x + 1) % X) * 2 + 1 - core], mate).wait_recv()
    to(7, out_ref.at[((x + 2) % X) * 2 + 1 - core], mate).wait_recv()

    for copy in (own_up, own_down, own_mate, on_up, left_mate, on_down, right_mate, far_mate):
        copy.wait_send()
    for hop in range(4):
        for copy in q_copies(hop) + up(hop) + down(hop):
            copy.wait_send()
    for i in range(8):
        for copy in direct(i) + first_leg(i) + second_leg(i):
            copy.wait_send()


def project_kernel(heads_ref, weight_ref, expand_ref, out_ref):
    total = dot(heads_ref[0], weight_ref[pl.ds(0, LANES), :])
    for t in range(1, 8):
        total = total + dot(heads_ref[t], weight_ref[pl.ds(t * LANES, LANES), :])
    total = total.astype(jnp.bfloat16)
    for p in range(PROBLEMS):
        out_ref[p * SPAN : (p + 1) * SPAN, :] = dot(
            expand_ref[p], total[p * LIVE : (p + 1) * LIVE]
        ).astype(jnp.bfloat16)


def per_device(queries, step_kv, tile_kv, tile_slot, step_lengths, parents, out_weight):
    bf16, f32 = jnp.bfloat16, jnp.float32
    smem = pl.BlockSpec(memory_space=pltpu.SMEM)
    vmem = pl.BlockSpec(memory_space=pltpu.VMEM)
    hbm = pl.BlockSpec(memory_space=pl.ANY)
    weights = lax.all_gather(out_weight, "dp", axis=0, tiled=True)

    send, qt, mask, expand, meta = pl.pallas_call(
        prep_kernel,
        out_shape=(
            jax.ShapeDtypeStruct((Y, Z, 2, 2, TILE, HD), bf16),
            jax.ShapeDtypeStruct((PROBLEMS, HD, LANES), bf16),
            jax.ShapeDtypeStruct((PROBLEMS, SPAN, LIVE), f32),
            jax.ShapeDtypeStruct((PROBLEMS, SPAN, LIVE), bf16),
            jax.ShapeDtypeStruct((256,), jnp.int32),
        ),
        in_specs=[smem, smem, smem, vmem, hbm],
        out_specs=(hbm, vmem, vmem, vmem, smem),
        scratch_shapes=[
            pltpu.SMEM((32,), jnp.int32),
            pltpu.SMEM((32,), jnp.int32),
            pltpu.SMEM((64,), jnp.int32),
            pltpu.SemaphoreType.DMA((32,)),
        ],
        compiler_params=pltpu.CompilerParams(vmem_limit_bytes=16 * MIB),
        cost_estimate=pl.CostEstimate(flops=100_000_000, bytes_accessed=20_000_000, transcendentals=0),
        name="prep",
    )(tile_slot, step_lengths, parents, queries, tile_kv)

    heads = pl.pallas_call(
        plane_kernel,
        out_shape=jax.ShapeDtypeStruct((8, PROBLEMS * LIVE, LANES), bf16),
        in_specs=[smem, hbm, vmem, vmem, vmem],
        out_specs=vmem,
        scratch_shapes=[pltpu.VMEM((8, 2, TILE, HD), bf16)] * 8
        + [pltpu.VMEM((PROBLEMS, HD, LANES), bf16)] * 7
        + [
            pltpu.VMEM((8, 2, 2, TILE, HD), bf16),
            pltpu.VMEM((9, HD, LANES), f32),
            pltpu.VMEM((9, 1, LANES), f32),
            pltpu.VMEM((9, 1, LANES), f32),
            pltpu.VMEM((PROBLEMS, HD, LANES), f32),
            pltpu.VMEM((PROBLEMS, 1, LANES), f32),
            pltpu.VMEM((PROBLEMS, 1, LANES), f32),
        ]
        + [
            pltpu.VMEM((4, PROBLEMS, HD, LANES), bf16),
            pltpu.VMEM((4, 8, LANES), f32),
        ]
        * 4
        + [
            pltpu.SemaphoreType.DMA((8,)),
            pltpu.SemaphoreType.DMA((8, 6)),
            pltpu.SemaphoreType.DMA((8, 6)),
            pltpu.SemaphoreType.DMA((4, 2)),
            pltpu.SemaphoreType.DMA((4, 2)),
            pltpu.SemaphoreType.DMA((4, 2, 2)),
            pltpu.SemaphoreType.DMA((4, 2, 2)),
            pltpu.SemaphoreType.DMA((8,)),
            pltpu.SemaphoreType.DMA((8,)),
        ],
        compiler_params=pltpu.CompilerParams(
            collective_id=0, has_side_effects=True, vmem_limit_bytes=56 * MIB
        ),
        cost_estimate=pl.CostEstimate(
            flops=60_000_000_000, bytes_accessed=300_000_000, transcendentals=10_000_000
        ),
        name="planes",
    )(meta, send, qt, step_kv, mask)

    columns = out_weight.shape[1]
    block = 256
    return pl.pallas_call(
        project_kernel,
        out_shape=jax.ShapeDtypeStruct((PROBLEMS * SPAN, columns), bf16),
        grid=(columns // block,),
        in_specs=[
            pl.BlockSpec((8, PROBLEMS * LIVE, LANES), lambda i: (0, 0, 0)),
            pl.BlockSpec((4096, block), lambda i: (0, i)),
            pl.BlockSpec((PROBLEMS, SPAN, LIVE), lambda i: (0, 0, 0)),
        ],
        out_specs=pl.BlockSpec((PROBLEMS * SPAN, block), lambda i: (0, i)),
        compiler_params=pltpu.CompilerParams(vmem_limit_bytes=32 * MIB),
        cost_estimate=pl.CostEstimate(
            flops=4_400_000_000, bytes_accessed=14_000_000, transcendentals=0
        ),
        name="project",
    )(heads, weights, expand)


def solution(mesh):
    return jax.shard_map(
        per_device,
        mesh=mesh,
        in_specs=(
            P("dp", "tensor"),
            P(None, "dp", "tensor"),
            P(None, "dp", "tensor"),
            P(),
            P(),
            P(),
            P("dp", "tensor"),
        ),
        out_specs=P("dp", "tensor"),
        check_vma=False,
    )
```

time: 416 us -> 228 us (0.55)
  waiting for transfers between devices: 271 us -> 0.73 us
  Pallas kernels: 0 us -> 195 us
  local copies, waits for them, and re-layouts: 69.4 us -> 16.5 us
  matrix products: 32.3 us -> 0 us
  other arithmetic: 13.5 us -> 0 us
  starting transfers between devices: 12 us -> 0.01 us
    all_to_all x1 -> x0, waiting for transfers between devices: 226 us -> none  [per_device(): lax.all_to_all(outgoing.reshape(2, senders, capacity, TILE, kv_width), 'd...]
    pallas_call x0 -> x3, Pallas kernels: none -> 195 us  [the longest x1 174 us: per_device(): pl.pallas_call(plane_kernel, out_shape=jax.ShapeDtypeStruct((8, PROBLEMS...]
    all_gather x2 -> x1, waiting for transfers between devices: 44.1 us -> 0.02 us  [per_device(): weights = lax.all_gather(out_weight, 'dp', axis=0, tiled=True)]
    dot_general x37 -> x0, matrix products: 32.3 us -> none  [the longest x1 12.1 us: per_device(): jnp.dot(lax.all_gather(head_out, 'tensor', axis=1, tiled=True), full_rows...]
    unnamed x13 -> x20, local copies, waits for them, and re-layouts: 0.19 us -> 16.5 us
    reshape x14 -> x0, local copies, waits for them, and re-layouts: 15.1 us -> none  [the longest x1 7.71 us: per_device(): outgoing.reshape(2, senders, capacity, TILE, kv_width)]
    all_to_all x1 -> x0, starting transfers between devices: 11.7 us -> none  [per_device(): lax.all_to_all(outgoing.reshape(2, senders, capacity, TILE, kv_width), 'd...]
    scatter x1 -> x0, local copies, waits for them, and re-layouts: 11.1 us -> none  [per_device(): outgoing = jnp.zeros((2, senders * capacity, TILE, kv_width), jnp.bfloat1...]
  transfers between devices with their start and end apart: 3 -> 1, of which waited for: 2 -> 0; matrix products, arithmetic and copies ran while one was open for 18% -> 1% of each run, Pallas kernels for 0% -> 83%
where the time goes in v1:
time: 228 us; the launch traced here: 226 us
  Pallas kernels  195 us (86%)
  local copies, waits for them, and re-layouts  16.5 us (7%)
  between operations  13.4 us (6%)
    pallas_call x1, Pallas kernels, per_device(): pl.pallas_call(plane_kernel, out_shape=jax.ShapeDtypeStruct((8, PROBLEMS...  174 us
    unnamed x20, local copies, waits for them, and re-layouts  16.5 us
    pallas_call x1, Pallas kernels, per_device(): pl.pallas_call(prep_kernel, out_shape=(jax.ShapeDtypeStruct((Y, Z, 2, 2,...  13.6 us
    pallas_call x1, Pallas kernels, per_device(): pl.pallas_call(project_kernel, out_shape=jax.ShapeDtypeStruct((PROBLEMS *...  8.16 us
  transfers between devices with their start and end apart: 1, of which 0 were waited for; matrix products, arithmetic and copies ran while one was open for 1% of the time, Pallas kernels for 83%

profile of v1, /device:TPU:6, one launch (start us, length us, event | category | flops | bytes accessed | tf_op | source)
XLA Modules:
  0.0 226.0 jit_solution(1558762601952437674)
XLA Ops:
  6.5 0.0 all-gather.2.cloned.1.call-start
  6.5 0.7 all-gather.2.cloned.1.call-update
  7.3 0.8 copy.8.length_ref
  8.0 0.8 copy.9.parent_ref
  8.8 0.0 copy-start
  8.8 2.2 copy-done
  11.0 0.0 copy-start.1
  11.0 1.1 copy-done.1
  12.2 0.0 copy-start.2
  12.2 0.7 copy-done.2
  12.8 13.6 %prep.1 = (bf16[4,8,2,2,256,128]{5,4,3,2,1,0:T(8,128)(2,1)S(1)}, bf16[4,128,512]{2,1,0:T(8,128)(2,1)S(1)}, f32[4,192,128]{2,1,0:T(8,128)S(1)}, bf16[4,192,128]{2,1,0:T(8,128)(2,1)S(1)}, s32[256]{0:T(256)S(1)}) custom-call(s32[1024]{0:T(1024)S(1)} %copy-done.2, s32[128,8]{1,0:T(8,128)S(1)} %copy.8.length_ref, s32[128,8]{1,0:T(8,128)S(1)} %copy.9.parent_ref, ...), custom_call_target="tpu_custom_call" | custom-call | flops 100000000 | bytes 20000000 | tf_op jit(solution)/shard_map/prep/pallas_call | solution.py:471
  26.5 0.0 copy-start.4
  26.5 3.2 %copy-done.4 = bf16[4,8,2,2,256,128]{5,4,3,2,1,0:T(8,128)(2,1)} copy-done((bf16[4,8,2,2,256,128]{5,4,3,2,1,0:T(8,128)(2,1)}, bf16[4,8,2,2,256,128]{5,4,3,2,1,0:T(8,128)(2,1)S(1)}, u32[]{:S(2)}) %copy-start.4) | copy-done | bytes 8388632
  29.7 0.0 copy-start.5
  29.7 0.8 copy-done.5
  30.5 0.0 copy-start.6
  30.5 0.8 copy-done.6
  31.3 0.0 copy-start.7
  31.3 0.6 copy-done.7
  31.8 173.6 %planes.1.heads_ref = bf16[8,512,512]{2,1,0:T(8,128)(2,1)} custom-call(s32[256]{0:T(256)} %copy-done.7, bf16[4,8,2,2,256,128]{5,4,3,2,1,0:T(8,128)(2,1)} %copy-done.4, bf16[4,128,512]{2,1,0:T(8,128)(2,1)} %copy-done.5, bf16[2,768,128]{2,1,0:T(8,128)(2,1)} %step_ref.1, f32[4,192,128]{2,1,0:T(8,128)} %copy-done.6), custom_call_target="tpu_custom_call" | custom-call | flops 60000002048 | bytes 300000000 | tf_op jit(solution)/shard_map/planes/pallas_call | solution.py:493
  205.4 0.0 all-gather.2.cloned.1.call-done.weight_ref
  205.4 0.0 copy-start.3
  205.4 3.4 %copy-done.3 = bf16[4096,1024]{1,0:T(8,128)(2,1)S(1)} copy-done((bf16[4096,1024]{1,0:T(8,128)(2,1)S(1)}, bf16[4096,1024]{1,0:T(8,128)(2,1)}, u32[]{:S(2)}) %copy-start.3) | copy-done | bytes 8388632
  208.8 0.0 copy-start.8
  208.8 2.2 copy-done.8
  211.0 8.2 %project.1 = bf16[768,1024]{1,0:T(8,128)(2,1)} custom-call(bf16[8,512,512]{2,1,0:T(8,128)(2,1)S(1)} %copy-done.8, bf16[4096,1024]{1,0:T(8,128)(2,1)S(1)} %copy-done.3, bf16[4,192,128]{2,1,0:T(8,128)(2,1)S(1)} %get-tuple-element.14.expand_ref), custom_call_target="tpu_custom_call" | custom-call | flops 4400000000 | bytes 14000000 | tf_op jit(solution)/shard_map/project/pallas_call | solution.py:536
Async XLA Ops:
  6.5 198.9 %all-gather.2.cloned.1.call-start = ((), (), s32[]{:S(2)}) async-start(), calls=%async_computation | async-start | bytes 8650752 | tf_op jit(solution)/shard_map/all_gather | solution.py:469
  8.8 2.2 copy-start
  11.0 1.1 copy-start.1
  12.2 0.7 copy-start.2
  26.5 3.2 %copy-start.4 = (bf16[4,8,2,2,256,128]{5,4,3,2,1,0:T(8,128)(2,1)}, bf16[4,8,2,2,256,128]{5,4,3,2,1,0:T(8,128)(2,1)S(1)}, u32[]{:S(2)}) copy-start(bf16[4,8,2,2,256,128]{5,4,3,2,1,0:T(8,128)(2,1)S(1)} %get-tuple-element.11.send_ref) | copy-start | bytes 25165828
  29.7 0.8 copy-start.5
  30.5 0.8 copy-start.6
  31.3 0.6 copy-start.7
  205.4 3.4 %copy-start.3 = (bf16[4096,1024]{1,0:T(8,128)(2,1)S(1)}, bf16[4096,1024]{1,0:T(8,128)(2,1)}, u32[]{:S(2)}) copy-start(bf16[4096,1024]{1,0:T(8,128)(2,1)} %all-gather.2.cloned.1.call-done.weight_ref) | copy-start | bytes 25165828
  208.8 2.2 copy-start.8
Sparse Core Ops, SparseCore 0:
  9.9 128.4 all-gather.1

commit v2 on v1

--- a/solution.py
+++ b/solution.py
@@ -25,11 +25,21 @@
 MESH = pl.DeviceIdType.MESH
 ORDER = (4, 3, 5, 2, 6, 1, 7, 0)
 MIB = 1 << 20
+VMEM = 60 * MIB
+HALF = 512
 
 META_ORDER = 0
 META_OWNER = 64
 META_SAME = 128
 META_LAST = 192
+META_SOURCE = 256
+
+
+class Pair:
+    def __init__(self, copy, leaving, arriving):
+        self.start = lambda: copy(leaving).start()
+        self.wait_send = lambda: copy(leaving).wait_send()
+        self.wait_recv = lambda: copy(arriving).wait_recv()
 
 
 def dot(a, b, dims=((1,), (0,))):
@@ -37,10 +47,23 @@
 
 
 def prep_kernel(
-    slot_ref, length_ref, parent_ref, query_ref, tile_ref,
-    send_ref, qt_ref, mask_ref, expand_ref, meta_ref,
-    count, count_in, owner_of, sems,
+    slot_hbm, length_hbm, parent_hbm, query_hbm,
+    qt_ref, mask_ref, expand_ref, meta_ref,
+    slot_ref, length_ref, parent_ref, query_ref, count, count_in, owner_of, sems,
 ):
+    loads = [
+        pltpu.make_async_copy(source, target, sems.at[i])
+        for i, (source, target) in enumerate(
+            (
+                (slot_hbm, slot_ref),
+                (length_hbm, length_ref),
+                (parent_hbm, parent_ref),
+                (query_hbm, query_ref),
+            )
+        )
+    ]
+    for load in loads:
+        load.start()
     dp = lax.axis_index("dp")
     z, y = dp // Y, dp % Y
 
@@ -57,9 +80,11 @@
         meta_ref[META_OWNER + i] = 0
         meta_ref[META_SAME + i] = 0
         meta_ref[META_LAST + i] = 0
+        meta_ref[META_SOURCE + i] = 0
         return 0
 
     lax.fori_loop(0, 64, clear_slots, 0)
+    loads[0].wait()
 
     def place(t, _):
         d = slot_ref[dp * 32 + t] >> 2
@@ -67,11 +92,7 @@
         r = ((d & 3) - y) & 3
         j = count[r * 8 + rz]
         count[r * 8 + rz] = j + 1
-        pltpu.make_async_copy(
-            tile_ref.at[:, pl.ds(pl.multiple_of(t * TILE, TILE), TILE), :],
-            send_ref.at[r, rz, j],
-            sems.at[t],
-        ).start()
+        meta_ref[META_SOURCE + rz * 8 + r * 2 + j] = t
         return 0
 
     lax.fori_loop(0, 32, place, 0)
@@ -115,14 +136,16 @@
 
     lax.fori_loop(0, 32, arrange, 0)
 
+    for load in loads[1:]:
+        load.wait()
     row = lax.broadcasted_iota(jnp.int32, (SPAN, LIVE), 0)
     lane = lax.broadcasted_iota(jnp.int32, (SPAN, LIVE), 1)
     step_of = row // STEP_LEN
     position = row - step_of * STEP_LEN
     for p in range(PROBLEMS):
         problem = dp * PROBLEMS + p
-        lengths = [length_ref[problem, s] for s in range(STEPS)]
-        links = [parent_ref[problem, s] for s in range(STEPS)]
+        lengths = [length_ref[s, problem] for s in range(STEPS)]
+        links = [parent_ref[s, problem] for s in range(STEPS)]
         starts, lines = [], []
         total = jnp.int32(0)
         for s in range(STEPS):
@@ -160,27 +183,20 @@
                 jnp.bfloat16
             )
 
-    def settle(t, _):
-        pltpu.make_async_copy(
-            tile_ref.at[:, pl.ds(0, TILE), :], send_ref.at[0, 0, 0], sems.at[t]
-        ).wait()
-        return 0
-
-    lax.fori_loop(0, 32, settle, 0)
-
 
 def plane_kernel(
-    meta_ref, send_ref, qt_ref, step_ref, mask_ref,
+    meta_ref, qt_hbm, mask_hbm, step_hbm, tile_hbm, weight_hbm,
     out_ref,
     *scratch,
 ):
     tiles = scratch[0:8]
-    qs = (qt_ref,) + tuple(scratch[8:15])
+    qs = scratch[8:16]
     (
+        mask_ref, step_ref, own_ref, send_ref, weights, heads,
         relay, state_o, state_m, state_l, step_o, step_m, step_l,
         up_in, up_in_s, up_out, up_out_s, down_in, down_in_s, down_out, down_out_s,
-        own_sem, y_send, y_recv, q_send, q_recv, c_send, c_recv, x_send, x_recv,
-    ) = scratch[15:]
+        own_sem, y_send, y_recv, q_send, q_recv, c_send, c_recv, x_send, x_recv, w_send, w_recv,
+    ) = scratch[16:]
     dp, tensor = lax.axis_index("dp"), lax.axis_index("tensor")
     z, y = dp // Y, dp % Y
     x, core = tensor // 2, tensor % 2
@@ -192,6 +208,22 @@
     x_down = (dp, ((x + X - 1) % X) * 2 + core)
     mate = (dp, x * 2 + 1 - core)
 
+    loads = [
+        pltpu.make_async_copy(source, target, own_sem.at[i])
+        for i, (source, target) in enumerate(
+            (
+                (qt_hbm, qs[0]),
+                (tile_hbm, own_ref),
+                (weight_hbm.at[:, pl.ds(0, HALF)], weights.at[0, z, y]),
+                (weight_hbm.at[:, pl.ds(HALF, HALF)], weights.at[1, z, y]),
+                (step_hbm, step_ref),
+                (mask_hbm, mask_ref),
+            )
+        )
+    ]
+    for load in loads:
+        load.start()
+
     barrier = pltpu.get_barrier_semaphore()
     peers = (y_up, y_down, z_up, z_down, x_up, x_down, mate)
     for peer in peers:
@@ -219,15 +251,14 @@
     def direct(i):
         rz = ORDER[i]
         return (
-            remote(send_ref.at[1, rz], tiles[rz].at[pl.ds(2, 2)], y_send.at[i, 0], y_recv.at[i, 0], y_up),
-            remote(send_ref.at[3, rz], tiles[rz].at[pl.ds(6, 2)], y_send.at[i, 1], y_recv.at[i, 1], y_down),
+            remote(send_ref.at[i, pl.ds(0, 2)], tiles[rz].at[pl.ds(2, 2)], y_send.at[i, 0], y_recv.at[i, 0], y_up),
+            remote(send_ref.at[i, pl.ds(4, 2)], tiles[rz].at[pl.ds(6, 2)], y_send.at[i, 1], y_recv.at[i, 1], y_down),
         )
 
     def first_leg(i):
-        rz = ORDER[i]
         return (
-            remote(send_ref.at[2, rz, 0], relay.at[i, 0], y_send.at[i, 2], y_recv.at[i, 2], y_up),
-            remote(send_ref.at[2, rz, 1], relay.at[i, 1], y_send.at[i, 3], y_recv.at[i, 3], y_down),
+            remote(send_ref.at[i, 2], relay.at[i, 0], y_send.at[i, 2], y_recv.at[i, 2], y_up),
+            remote(send_ref.at[i, 3], relay.at[i, 1], y_send.at[i, 3], y_recv.at[i, 3], y_down),
         )
 
     def second_leg(i):
@@ -237,9 +268,64 @@
             remote(relay.at[i, 1], tiles[rz].at[5], y_send.at[i, 5], y_recv.at[i, 5], y_down),
         )
 
-    def own(i):
+    def pack(i):
         rz = ORDER[i]
-        return pltpu.make_async_copy(send_ref.at[0, rz], tiles[rz].at[pl.ds(0, 2)], own_sem.at[i])
+
+        def keep(s, _):
+            tiles[rz][s] = own_ref[:, meta_ref[META_SOURCE + rz * 8 + s]]
+            return 0
+
+        def give(s, _):
+            send_ref[i, s] = own_ref[:, meta_ref[META_SOURCE + rz * 8 + 2 + s]]
+            return 0
+
+        lax.fori_loop(0, 2, keep, 0)
+        lax.fori_loop(0, 6, give, 0)
+
+    def along_z(view, low, high, k, hop):
+        up_block, down_block = view((z + Z - hop) % Z), view((z + hop) % Z)
+        up_next, down_next = view((z + Z - hop - 1) % Z), view((z + hop + 1) % Z)
+        if hop == 3:
+            up_block, up_next = up_block.at[low], up_next.at[low]
+            down_block, down_next = down_block.at[high], down_next.at[high]
+        return ring_pair(up_block, up_next, z_up, down_block, down_next, z_down, k + hop)
+
+    def along_y(view, low, high, k, hop):
+        up_block, down_block = view((y + Y - hop) % Y), view((y + hop) % Y)
+        up_next, down_next = view((y + Y - hop - 1) % Y), view((y + hop + 1) % Y)
+        if hop == 1:
+            up_block, up_next = up_block.at[low], up_next.at[low]
+            down_block, down_next = down_block.at[high], down_next.at[high]
+        return ring_pair(up_block, up_next, y_up, down_block, down_next, y_down, k + hop)
+
+    def ring_pair(up_block, up_next, up_peer, down_block, down_next, down_peer, k):
+        def side(i, peer):
+            return lambda block: remote(block, block, w_send.at[k, i], w_recv.at[k, i], peer)
+
+        return (
+            Pair(side(0, up_peer), up_block, up_next),
+            Pair(side(1, down_peer), down_block, down_next),
+        )
+
+    first_rows, last_rows = pl.ds(0, HD // 2), pl.ds(HD // 2, HD // 2)
+
+    def a1(hop):
+        return along_y(lambda k: weights.at[0, z, k], first_rows, last_rows, 0, hop)
+
+    def a2(hop):
+        return along_z(lambda k: weights.at[0, k], pl.ds(0, 2), pl.ds(2, 2), 2, hop)
+
+    def b1(hop):
+        return along_z(lambda k: weights.at[1, k, y], first_rows, last_rows, 6, hop)
+
+    def b2(hop):
+        view = lambda k: weights.at[1, :, k]
+        if hop == 0:
+            return along_y(view, None, None, 10, 0)
+        halves = pl.ds(0, 4), pl.ds(4, 4)
+        up_block, down_block = weights.at[1, halves[0], (y + Y - 1) % Y], weights.at[1, halves[1], (y + 1) % Y]
+        up_next, down_next = weights.at[1, halves[0], (y + 2) % Y], weights.at[1, halves[1], (y + 2) % Y]
+        return ring_pair(up_block, up_next, y_up, down_block, down_next, y_down, 11)
 
     def start(copies):
         for copy in copies:
@@ -253,13 +339,18 @@
         arrived(first_leg(i))
         start(second_leg(i))
 
+    loads[0].wait()
     start(q_copies(0))
+    loads[2].wait()
+    loads[3].wait()
+    start(a1(0))
+    start(b1(0))
+    loads[1].wait()
     for i in range(4):
+        pack(i)
         start(first_leg(i))
         if i < 3:
             start(direct(i))
-    for i in range(8):
-        own(i).start()
 
     state_o[0] = jnp.zeros((HD, LANES), jnp.float32)
     state_m[0] = jnp.full((1, LANES), LOW, jnp.float32)
@@ -274,7 +365,7 @@
         rows = pl.ds(pl.multiple_of(p * SPAN, SPAN), SPAN)
         mask = mask_ref[p]
         mask = jnp.concatenate([mask] * GROUP, axis=1)
-        scores = dot(step_ref[0, rows, :], qt_ref[p]) * SCALE
+        scores = dot(step_ref[0, rows, :], qs[0][p]) * SCALE
         scores = jnp.where(mask > 0.5, scores, LOW)
         m, l, weights = soften(scores, jnp.full((1, LANES), LOW, jnp.float32))
         step_o[p] = dot(step_ref[1, rows, :], weights, ((0,), (0,)))
@@ -361,20 +452,32 @@
         arrived(q_copies(hop))
         start(q_copies(hop + 1))
         pass_on(hop)
+        arrived(b1(hop))
+        start(b1(hop + 1))
+        if hop == 0:
+            arrived(a1(0))
+            start(a1(1))
+    loads[4].wait()
+    loads[5].wait()
     lax.fori_loop(0, PROBLEMS, attend_steps, 0)
+    arrived(a1(1))
 
     for i in range(8):
         rz = ORDER[i]
         arrived(direct(i))
         arrived(second_leg(i))
-        own(i).wait()
         if i + 3 < 8:
             start(direct(i + 3))
             if i + 4 < 8:
+                pack(i + 4)
                 start(first_leg(i + 4))
             pass_on(i + 3)
         if i == 0:
             arrived(q_copies(3))
+            arrived(b1(3))
+            start(a2(0))
+        if i == 5:
+            start(b2(0))
         attend_tiles(rz)
         if rz == 4:
             pass_sums(0, rz, 0)
@@ -383,6 +486,9 @@
             pass_sums(4 - rz, rz, 0)
         elif rz in (5, 6, 7):
             pass_sums(rz - 4, rz, 1)
+        if i in (2, 4, 6):
+            arrived(a2(i // 2 - 1))
+            start(a2(i // 2))
     arrived(up(3))
     arrived(down(3))
 
@@ -403,7 +509,7 @@
         rows = pl.ds(pl.multiple_of(p * LIVE, LIVE), LIVE)
         for h in range(GROUP):
             block = result[:, h * LIVE : (h + 1) * LIVE]
-            out_ref[mine, rows, h * HD : (h + 1) * HD] = block.T.astype(jnp.bfloat16)
+            heads[mine, rows, h * HD : (h + 1) * HD] = block.T.astype(jnp.bfloat16)
         return 0
 
     lax.fori_loop(0, PROBLEMS, finish, 0)
@@ -417,87 +523,117 @@
     def to(k, view, peer):
         return remote(view, view, x_send.at[k], x_recv.at[k], peer)
 
-    own_up = to(0, out_ref.at[mine], x_up)
-    own_down = to(1, out_ref.at[mine], x_down)
-    own_mate = to(2, out_ref.at[mine], mate)
+    own_up = to(0, heads.at[mine], x_up)
+    own_down = to(1, heads.at[mine], x_down)
+    own_mate = to(2, heads.at[mine], mate)
     start((own_up, own_down, own_mate))
-    from_left = to(0, out_ref.at[left], x_up)
-    from_right = to(1, out_ref.at[right], x_down)
+    from_left = to(0, heads.at[left], x_up)
+    from_right = to(1, heads.at[right], x_down)
     from_left.wait_recv()
-    on_up = to(3, out_ref.at[left, low], x_up)
-    left_mate = to(4, out_ref.at[left], mate)
+    on_up = to(3, heads.at[left, low], x_up)
+    left_mate = to(4, heads.at[left], mate)
     start((on_up, left_mate))
     from_right.wait_recv()
-    on_down = to(5, out_ref.at[right, high], x_down)
-    right_mate = to(6, out_ref.at[right], mate)
+    on_down = to(5, heads.at[right, high], x_down)
+    right_mate = to(6, heads.at[right], mate)
     start((on_down, right_mate))
-    to(3, out_ref.at[far, low], x_up).wait_recv()
-    to(5, out_ref.at[far, high], x_down).wait_recv()
-    far_mate = to(7, out_ref.at[far], mate)
+    arrived(b2(0))
+    start(b2(1))
+    to(3, heads.at[far, low], x_up).wait_recv()
+    to(5, heads.at[far, high], x_down).wait_recv()
+    far_mate = to(7, heads.at[far], mate)
     far_mate.start()
-    to(2, out_ref.at[x * 2 + 1 - core], mate).wait_recv()
-    to(4, out_ref.at[((x + X - 1) % X) * 2 + 1 - core], mate).wait_recv()
-    to(6, out_ref.at[((x + 1) % X) * 2 + 1 - core], mate).wait_recv()
-    to(7, out_ref.at[((x + 2) % X) * 2 + 1 - core], mate).wait_recv()
+    to(2, heads.at[x * 2 + 1 - core], mate).wait_recv()
+    to(4, heads.at[((x + X - 1) % X) * 2 + 1 - core], mate).wait_recv()
+    to(6, heads.at[((x + 1) % X) * 2 + 1 - core], mate).wait_recv()
+    to(7, heads.at[((x + 2) % X) * 2 + 1 - core], mate).wait_recv()
+
+    def project(half):
+        def block(c, _):
+            columns = pl.ds(pl.multiple_of(c * 256, 256), 256)
+            total = jnp.zeros((ROWS, 256), jnp.float32)
+            for t in range(8):
+                block = weights[half, t, :, :, columns].reshape(LANES, 256)
+                total = total + dot(heads[t], block)
+            into = pl.ds(pl.multiple_of(half * HALF + c * 256, 256), 256)
+            out_ref[:, into] = total.astype(jnp.bfloat16)
+            return 0
+
+        lax.fori_loop(0, HALF // 256, block, 0)
+
+    arrived(a2(3))
+    project(0)
+    arrived(b2(1))
+    project(1)
 
     for copy in (own_up, own_down, own_mate, on_up, left_mate, on_down, right_mate, far_mate):
         copy.wait_send()
     for hop in range(4):
         for copy in q_copies(hop) + up(hop) + down(hop):
             copy.wait_send()
+        for copy in a2(hop) + b1(hop):
+            copy.wait_send()
+    for hop in range(2):
+        for copy in a1(hop) + b2(hop):
+            copy.wait_send()
     for i in range(8):
         for copy in direct(i) + first_leg(i) + second_leg(i):
             copy.wait_send()
 
 
-def project_kernel(heads_ref, weight_ref, expand_ref, out_ref):
-    total = dot(heads_ref[0], weight_ref[pl.ds(0, LANES), :])
-    for t in range(1, 8):
-        total = total + dot(heads_ref[t], weight_ref[pl.ds(t * LANES, LANES), :])
-    total = total.astype(jnp.bfloat16)
+def expand_kernel(compact_ref, expand_ref, out_ref):
     for p in range(PROBLEMS):
         out_ref[p * SPAN : (p + 1) * SPAN, :] = dot(
-            expand_ref[p], total[p * LIVE : (p + 1) * LIVE]
+            expand_ref[p], compact_ref[p * LIVE : (p + 1) * LIVE, :]
         ).astype(jnp.bfloat16)
 
 
 def per_device(queries, step_kv, tile_kv, tile_slot, step_lengths, parents, out_weight):
-    bf16, f32 = jnp.bfloat16, jnp.float32
+    bf16, f32, i32 = jnp.bfloat16, jnp.float32, jnp.int32
     smem = pl.BlockSpec(memory_space=pltpu.SMEM)
     vmem = pl.BlockSpec(memory_space=pltpu.VMEM)
     hbm = pl.BlockSpec(memory_space=pl.ANY)
-    weights = lax.all_gather(out_weight, "dp", axis=0, tiled=True)
-
-    send, qt, mask, expand, meta = pl.pallas_call(
+    columns = out_weight.shape[1]
+
+    qt, mask, expand, meta = pl.pallas_call(
         prep_kernel,
         out_shape=(
-            jax.ShapeDtypeStruct((Y, Z, 2, 2, TILE, HD), bf16),
             jax.ShapeDtypeStruct((PROBLEMS, HD, LANES), bf16),
             jax.ShapeDtypeStruct((PROBLEMS, SPAN, LIVE), f32),
             jax.ShapeDtypeStruct((PROBLEMS, SPAN, LIVE), bf16),
-            jax.ShapeDtypeStruct((256,), jnp.int32),
+            jax.ShapeDtypeStruct((512,), i32),
         ),
-        in_specs=[smem, smem, smem, vmem, hbm],
-        out_specs=(hbm, vmem, vmem, vmem, smem),
+        in_specs=[hbm] * 4,
+        out_specs=(vmem, vmem, vmem, smem),
         scratch_shapes=[
-            pltpu.SMEM((32,), jnp.int32),
-            pltpu.SMEM((32,), jnp.int32),
-            pltpu.SMEM((64,), jnp.int32),
-            pltpu.SemaphoreType.DMA((32,)),
+            pltpu.SMEM((1024,), i32),
+            pltpu.SMEM((STEPS, 128), i32),
+            pltpu.SMEM((STEPS, 128), i32),
+            pltpu.VMEM(queries.shape, bf16),
+            pltpu.SMEM((32,), i32),
+            pltpu.SMEM((32,), i32),
+            pltpu.SMEM((64,), i32),
+            pltpu.SemaphoreType.DMA((4,)),
         ],
-        compiler_params=pltpu.CompilerParams(vmem_limit_bytes=16 * MIB),
-        cost_estimate=pl.CostEstimate(flops=100_000_000, bytes_accessed=20_000_000, transcendentals=0),
+        compiler_params=pltpu.CompilerParams(vmem_limit_bytes=VMEM),
+        cost_estimate=pl.CostEstimate(flops=100_000_000, bytes_accessed=4_000_000, transcendentals=0),
         name="prep",
-    )(tile_slot, step_lengths, parents, queries, tile_kv)
-
-    heads = pl.pallas_call(
+    )(tile_slot, step_lengths.T, parents.T, queries)
+
+    compact = pl.pallas_call(
         plane_kernel,
-        out_shape=jax.ShapeDtypeStruct((8, PROBLEMS * LIVE, LANES), bf16),
-        in_specs=[smem, hbm, vmem, vmem, vmem],
+        out_shape=jax.ShapeDtypeStruct((PROBLEMS * LIVE, columns), bf16),
+        in_specs=[smem] + [hbm] * 5,
         out_specs=vmem,
         scratch_shapes=[pltpu.VMEM((8, 2, TILE, HD), bf16)] * 8
-        + [pltpu.VMEM((PROBLEMS, HD, LANES), bf16)] * 7
+        + [pltpu.VMEM((PROBLEMS, HD, LANES), bf16)] * 8
         + [
+            pltpu.VMEM((PROBLEMS, SPAN, LIVE), f32),
+            pltpu.VMEM(step_kv.shape, bf16),
+            pltpu.VMEM((2, 32, TILE, HD), bf16),
+            pltpu.VMEM((8, 6, 2, TILE, HD), bf16),
+            pltpu.VMEM((2, Z, Y, HD, HALF), bf16),
+            pltpu.VMEM((8, PROBLEMS * LIVE, LANES), bf16),
             pltpu.VMEM((8, 2, 2, TILE, HD), bf16),
             pltpu.VMEM((9, HD, LANES), f32),
             pltpu.VMEM((9, 1, LANES), f32),
@@ -521,34 +657,34 @@
             pltpu.SemaphoreType.DMA((4, 2, 2)),
             pltpu.SemaphoreType.DMA((8,)),
             pltpu.SemaphoreType.DMA((8,)),
+            pltpu.SemaphoreType.DMA((12, 2)),
+            pltpu.SemaphoreType.DMA((12, 2)),
         ],
         compiler_params=pltpu.CompilerParams(
-            collective_id=0, has_side_effects=True, vmem_limit_bytes=56 * MIB
+            collective_id=0, has_side_effects=True, vmem_limit_bytes=VMEM
         ),
         cost_estimate=pl.CostEstimate(
             flops=60_000_000_000, bytes_accessed=300_000_000, transcendentals=10_000_000
         ),
         name="planes",
-    )(meta, send, qt, step_kv, mask)
-
-    columns = out_weight.shape[1]
-    block = 256
+    )(meta, qt, mask, step_kv, tile_kv.reshape(2, 32, TILE, HD), out_weight)
+
+    block = 512
     return pl.pallas_call(
-        project_kernel,
+        expand_kernel,
         out_shape=jax.ShapeDtypeStruct((PROBLEMS * SPAN, columns), bf16),
         grid=(columns // block,),
         in_specs=[
-            pl.BlockSpec((8, PROBLEMS * LIVE, LANES), lambda i: (0, 0, 0)),
-            pl.BlockSpec((4096, block), lambda i: (0, i)),
+            pl.BlockSpec((PROBLEMS * LIVE, block), lambda i: (0, i)),
             pl.BlockSpec((PROBLEMS, SPAN, LIVE), lambda i: (0, 0, 0)),
         ],
         out_specs=pl.BlockSpec((PROBLEMS * SPAN, block), lambda i: (0, i)),
-        compiler_params=pltpu.CompilerParams(vmem_limit_bytes=32 * MIB),
+        compiler_params=pltpu.CompilerParams(vmem_limit_bytes=VMEM),
         cost_estimate=pl.CostEstimate(
-            flops=4_400_000_000, bytes_accessed=14_000_000, transcendentals=0
+            flops=200_000_000, bytes_accessed=3_000_000, transcendentals=0
         ),
-        name="project",
-    )(heads, weights, expand)
+        name="expand",
+    )(compact, expand)
 
 
 def solution(mesh):

time: 228 us -> 182 us (0.80)
  local copies, waits for them, and re-layouts: 16.5 us -> 0 us
  Pallas kernels: 195 us -> 179 us
  between operations: 13.4 us -> 0.02 us
    pallas_call x3, Pallas kernels: 195 us -> 179 us  [the longest x1 168 us: per_device(): pl.pallas_call(plane_kernel, out_shape=jax.ShapeDtypeStruct((PROBLEMS * L...]
    unnamed x20 -> x0, local copies, waits for them, and re-layouts: 16.5 us -> none
  transfers between devices with their start and end apart: 1 -> 0, of which waited for: 0 -> 0; matrix products, arithmetic and copies ran while one was open for 1% -> 0% of each run, Pallas kernels for 83% -> 0%
where the time goes in v2:
time: 182 us; the launch traced here: 179 us
  Pallas kernels  179 us (98%)
    pallas_call x1, Pallas kernels, per_device(): pl.pallas_call(plane_kernel, out_shape=jax.ShapeDtypeStruct((PROBLEMS * L...  168 us
    pallas_call x1, Pallas kernels, per_device(): pl.pallas_call(prep_kernel, out_shape=(jax.ShapeDtypeStruct((PROBLEMS, HD...  7.87 us

profile of v2, /device:TPU:6, one launch (start us, length us, event | category | flops | bytes accessed | tf_op | source)
XLA Modules:
  0.0 178.7 jit_solution(17997514534488891778)
XLA Ops:
  0.0 7.9 %prep.1 = (bf16[4,128,512]{2,1,0:T(8,128)(2,1)}, f32[4,192,128]{2,1,0:T(8,128)}, bf16[4,192,128]{2,1,0:T(8,128)(2,1)}, s32[512]{0:T(512)}) custom-call(s32[1024]{0:T(1024)} %slot_hbm.1, s32[8,128]{1,0:T(8,128)} %bitcast.3, s32[8,128]{1,0:T(8,128)} %bitcast.4, bf16[768,512]{1,0:T(8,128)(2,1)} %query_hbm.1), custom_call_target="tpu_custom_call" | custom-call | flops 100000000 | bytes 4000000 | tf_op jit(solution)/shard_map/prep/pallas_call | solution.py:598
  7.9 168.1 %planes.1.compact_ref = bf16[512,1024]{1,0:T(8,128)(2,1)} custom-call(s32[512]{0:T(512)} %get-tuple-element.9.meta_ref, bf16[4,128,512]{2,1,0:T(8,128)(2,1)} %get-tuple-element.10.qt_hbm, f32[4,192,128]{2,1,0:T(8,128)} %get-tuple-element.11.mask_hbm, bf16[2,768,128]{2,1,0:T(8,128)(2,1)} %step_hbm.1, bf16[2,32,256,128]{3,2,1,0:T(8,128)(2,1)} %bitcast.5, ...), custom_call_target="tpu_custom_call" | custom-call | flops 60000002048 | bytes 300000000 | tf_op jit(solution)/shard_map/planes/pallas_call | solution.py:623
  176.0 2.7 %expand.1 = bf16[768,1024]{1,0:T(8,128)(2,1)} custom-call(bf16[512,1024]{1,0:T(8,128)(2,1)} %planes.1.compact_ref, bf16[4,192,128]{2,1,0:T(8,128)(2,1)} %get-tuple-element.12.expand_ref), custom_call_target="tpu_custom_call" | custom-call | flops 200000000 | bytes 3000000 | tf_op jit(solution)/shard_map/expand/pallas_call | solution.py:673

commit v3 on v2

v3 whole, which is shorter than its diff:
```python
import functools
import math

import jax
import jax.numpy as jnp
from jax import lax
from jax.experimental import pallas as pl
from jax.experimental.pallas import tpu as pltpu
from jax.sharding import PartitionSpec as P

HD = 128
TILE = 256
STEPS = 8
STEP_LEN = 24
SPAN = STEPS * STEP_LEN
PROBLEMS = 4
GROUP = 4
LIVE = 128
LANES = GROUP * LIVE
Z = 8
Y = 4
X = 4
LOW = -1e30
SCALE = math.log2(math.e) / math.sqrt(HD)
MESH = pl.DeviceIdType.MESH
ORDER = (4, 3, 5, 2, 6, 1, 7, 0)
MIB = 1 << 20
VMEM = 60 * MIB
PART_A = 256
PART_B = 768
HALVES = ((2, 4), (0, 2))
AHEAD = 4
B2_TURN = 3

META_ORDER = 0
META_OWNER = 64
META_SAME = 128
META_LAST = 192
META_SOURCE = 256
CAPACITIES = (12, 13, 16)


class Pair:
    def __init__(self, copy, leaving, arriving):
        self.start = lambda: copy(leaving).start()
        self.wait_send = lambda: copy(leaving).wait_send()
        self.wait_recv = lambda: copy(arriving).wait_recv()


def dot(a, b, dims=((1,), (0,))):
    return lax.dot_general(a, b, (dims, ((), ())), preferred_element_type=jnp.float32)


def prep_kernel(
    slot_hbm, table_hbm, length_hbm, parent_hbm, query_hbm,
    qt_ref, mask_ref, expand_ref, meta_ref, choice_ref,
    slot_ref, table_ref, length_ref, parent_ref, query_ref,
    count, count_in, rank, given, taken, place_of, sems,
):
    loads = [
        pltpu.make_async_copy(source, target, sems.at[i])
        for i, (source, target) in enumerate(
            (
                (slot_hbm, slot_ref),
                (table_hbm, table_ref),
                (length_hbm, length_ref),
                (parent_hbm, parent_ref),
                (query_hbm, query_ref),
            )
        )
    ]
    for load in loads:
        load.start()
    dp = lax.axis_index("dp")
    z, y = dp // Y, dp % Y

    def clear(i, _):
        count[i] = 0
        count_in[i] = 0
        return 0

    lax.fori_loop(0, 32, clear, 0)

    def clear_slots(i, _):
        given[i] = -1
        taken[i] = -1
        meta_ref[META_ORDER + i] = 0
        meta_ref[META_OWNER + i] = 0
        meta_ref[META_SAME + i] = 0
        meta_ref[META_LAST + i] = 0
        meta_ref[META_SOURCE + i] = 0
        return 0

    lax.fori_loop(0, 64, clear_slots, 0)
    for i, rz in enumerate(ORDER):
        rank[rz] = i
    loads[0].wait()

    def place(t, _):
        d = slot_ref[dp * 32 + t] >> 2
        turn = rank[((d >> 2) - z) & 7]
        r = ((d & 3) - y) & 3
        j = count[r * 8 + turn]
        count[r * 8 + turn] = j + 1
        given[r * 16 + turn * 2 + j] = t
        return 0

    lax.fori_loop(0, 32, place, 0)

    def arrive(q, _):
        s = slot_ref[z * 128 + q]
        d = s >> 2

        @pl.when((d & 3) == y)
        def _():
            turn = rank[((d >> 2) - z) & 7]
            r = (y - (q >> 5)) & 3
            j = count_in[r * 8 + turn]
            count_in[r * 8 + turn] = j + 1
            taken[r * 16 + turn * 2 + j] = s & 3

        return 0

    lax.fori_loop(0, 128, arrive, 0)

    def close(i, carry):
        sent, got = carry
        sent, got = jnp.where(i % 16 == 0, 0, sent), jnp.where(i % 16 == 0, 0, got)
        base = (i // 16) * 16
        tile = given[i]
        give, take = tile >= 0, taken[i] >= 0

        @pl.when(give)
        def _():
            meta_ref[META_SOURCE + base + sent] = tile

        place_of[i] = base + got
        return sent + give.astype(jnp.int32), got + take.astype(jnp.int32)

    lax.fori_loop(0, 64, close, (0, 0))

    def arrange(i, n):
        turn, p = i // 4, i % 4
        n = jnp.where(p == 0, 0, n)

        def scan(s, carry):
            n, seen = carry
            index = (s // 2) * 16 + turn * 2 + s % 2
            match = taken[index] == p

            @pl.when(match)
            def _():
                meta_ref[META_ORDER + turn * 8 + n] = place_of[index]
                meta_ref[META_OWNER + turn * 8 + n] = p
                meta_ref[META_SAME + turn * 8 + n] = seen
                meta_ref[META_LAST + turn * 4 + p] = n + 1

            hit = match.astype(jnp.int32)
            return n + hit, jnp.maximum(seen, hit)

        n, _ = lax.fori_loop(0, 8, scan, (n, 0))
        return n

    lax.fori_loop(0, 32, arrange, 0)

    for load in loads[1:]:
        load.wait()

    table = table_ref[...]
    column = (table >> 2) & 3
    lane = lax.broadcasted_iota(jnp.int32, (8, 128), 1) // 32
    block = lax.broadcasted_iota(jnp.int32, (128, 128), 0) // 32
    same_block = block == lax.broadcasted_iota(jnp.int32, (128, 128), 1) // 32
    ones = jnp.where(same_block, 1.0, 0.0).astype(jnp.bfloat16)
    most = jnp.zeros((8, 128), jnp.float32)
    for v in range(Y):
        hit = jnp.where((column == v) & (lane != v), 1.0, 0.0).astype(jnp.bfloat16)
        most = jnp.maximum(most, dot(hit, ones))
    most = jnp.max(most)
    choice = jnp.int32(0)
    for capacity in CAPACITIES[:-1]:
        choice = choice + (most > capacity + 0.5).astype(jnp.int32)
    choice_ref[0] = choice

    row = lax.broadcasted_iota(jnp.int32, (SPAN, LIVE), 0)
    lane = lax.broadcasted_iota(jnp.int32, (SPAN, LIVE), 1)
    step_of = row // STEP_LEN
    position = row - step_of * STEP_LEN
    for p in range(PROBLEMS):
        problem = dp * PROBLEMS + p
        lengths = [length_ref[s, problem] for s in range(STEPS)]
        links = [parent_ref[s, problem] for s in range(STEPS)]
        starts, lines = [], []
        total = jnp.int32(0)
        for s in range(STEPS):
            starts.append(total)
            total = total + lengths[s]
            line = jnp.int32(1 << s)
            for b in range(s):
                line = line | jnp.where(links[s] == b, lines[b], 0)
            lines.append(line)
        row_start, row_length = jnp.zeros_like(row), jnp.zeros_like(row)
        row_bit = jnp.zeros_like(row)
        lane_step, lane_start, lane_line = jnp.zeros_like(row), jnp.zeros_like(row), jnp.zeros_like(row)
        for s in range(STEPS):
            here = step_of == s
            row_start = jnp.where(here, starts[s], row_start)
            row_length = jnp.where(here, lengths[s], row_length)
            row_bit = jnp.where(here, 1 << s, row_bit)
            passed = lane >= starts[s]
            lane_step = jnp.where(passed, s, lane_step)
            lane_start = jnp.where(passed, starts[s], lane_start)
            lane_line = jnp.where(passed, lines[s], lane_line)
        live = position < row_length
        picked = (lane == row_start + position) & live
        expand = jnp.where(picked, 1.0, 0.0).astype(jnp.bfloat16)
        expand_ref[p] = expand
        visible = (
            ((lane_line & row_bit) != 0)
            & live
            & ((step_of != lane_step) | (position <= lane - lane_start))
        )
        mask_ref[p] = jnp.where(visible, 1.0, 0.0)
        for h in range(GROUP):
            block = query_ref[p * SPAN : (p + 1) * SPAN, h * HD : (h + 1) * HD]
            qt_ref[p, :, h * LIVE : (h + 1) * LIVE] = dot(block, expand, ((0,), (0,))).astype(
                jnp.bfloat16
            )


def plane_kernel(
    capacity,
    meta_ref, qt_hbm, mask_hbm, step_hbm, tile_hbm, weight_hbm,
    out_ref,
    *scratch,
):
    qs = scratch[0:8]
    (
        mask_ref, step_ref, own_ref, send_ref, here_ref, pool_ref, weights_a, weights_b, heads,
        relay, state_o, state_m, state_l, step_o, step_m, step_l,
        up_in, up_in_s, up_out, up_out_s, down_in, down_in_s, down_out, down_out_s,
        total_b, own_sem, y_send, y_recv, q_send, q_recv, c_send, c_recv, x_send, x_recv, w_send, w_recv,
    ) = scratch[8:]
    chunks = (capacity + 1) // 2
    dp, tensor = lax.axis_index("dp"), lax.axis_index("tensor")
    z, y = dp // Y, dp % Y
    x, core = tensor // 2, tensor % 2
    y_up = (z * Y + (y + 1) % Y, tensor)
    y_down = (z * Y + (y + Y - 1) % Y, tensor)
    z_up = (((z + 1) % Z) * Y + y, tensor)
    z_down = (((z + Z - 1) % Z) * Y + y, tensor)
    x_up = (dp, ((x + 1) % X) * 2 + core)
    x_down = (dp, ((x + X - 1) % X) * 2 + core)
    mate = (dp, x * 2 + 1 - core)

    loads = [
        pltpu.make_async_copy(source, target, own_sem.at[i])
        for i, (source, target) in enumerate(
            (
                (qt_hbm, qs[0]),
                (tile_hbm, own_ref),
                (weight_hbm.at[:, pl.ds(0, PART_A)], weights_a.at[z, y]),
                (weight_hbm.at[:, pl.ds(PART_A, PART_B)], weights_b.at[z, y]),
                (step_hbm, step_ref),
                (mask_hbm, mask_ref),
            )
        )
    ]
    for load in loads:
        load.start()

    barrier = pltpu.get_barrier_semaphore()
    peers = (y_up, y_down, z_up, z_down, x_up, x_down, mate)
    for peer in peers:
        pl.semaphore_signal(barrier, inc=1, device_id=peer, device_id_type=MESH)
    pl.semaphore_wait(barrier, len(peers))

    def remote(src, dst, send_sem, recv_sem, peer):
        return pltpu.make_async_remote_copy(
            src_ref=src, dst_ref=dst, send_sem=send_sem, recv_sem=recv_sem,
            device_id=peer, device_id_type=MESH,
        )

    def q_copies(hop):
        up_from, up_to = (8 - hop) % 8, 7 - hop
        up_src, up_dst = qs[up_from], qs[up_to]
        down_src, down_dst = qs[hop], qs[hop + 1]
        if hop == 3:
            up_src, up_dst = up_src.at[pl.ds(0, 2)], up_dst.at[pl.ds(0, 2)]
            down_src, down_dst = down_src.at[pl.ds(2, 2)], down_dst.at[pl.ds(2, 2)]
        return (
            remote(up_src, up_dst, q_send.at[hop, 0], q_recv.at[hop, 0], z_up),
            remote(down_src, down_dst, q_send.at[hop, 1], q_recv.at[hop, 1], z_down),
        )

    def span(i):
        return pl.ds(2 * i, min(2, capacity - 2 * i))

    def direct(i):
        at = span(i)
        return (
            remote(send_ref.at[0, at], here_ref.at[0, at], y_send.at[i, 0], y_recv.at[i, 0], y_up),
            remote(send_ref.at[2, at], here_ref.at[2, at], y_send.at[i, 1], y_recv.at[i, 1], y_down),
        )

    def first_leg(i):
        at = span(i)
        return (
            remote(send_ref.at[1, at, 0], relay.at[0, at], y_send.at[i, 2], y_recv.at[i, 2], y_up),
            remote(send_ref.at[1, at, 1], relay.at[1, at], y_send.at[i, 3], y_recv.at[i, 3], y_down),
        )

    def second_leg(i):
        at = span(i)
        return (
            remote(relay.at[0, at], here_ref.at[1, at, 0], y_send.at[i, 4], y_recv.at[i, 4], y_up),
            remote(relay.at[1, at], here_ref.at[1, at, 1], y_send.at[i, 5], y_recv.at[i, 5], y_down),
        )

    def pack(i):
        def give(k, _):
            for r in range(1, Y):
                send_ref[r - 1, k] = own_ref[:, meta_ref[META_SOURCE + r * 16 + k]]
            return 0

        lax.fori_loop(2 * i, min(2 * i + 2, capacity), give, 0)

    def keep(k, _):
        pool_ref[k] = own_ref[:, meta_ref[META_SOURCE + k]]
        return 0

    def join(i):
        arrived(direct(i))
        arrived(second_leg(i))
        for r in range(1, Y):
            for k in range(2 * i, min(2 * i + 2, capacity)):
                pool_ref[r * 16 + k] = here_ref[r - 1, k]

    def along_z(view, low, high, k, hop):
        up_block, down_block = view((z + Z - hop) % Z), view((z + hop) % Z)
        up_next, down_next = view((z + Z - hop - 1) % Z), view((z + hop + 1) % Z)
        if hop == 3:
            up_block, up_next = up_block.at[low], up_next.at[low]
            down_block, down_next = down_block.at[high], down_next.at[high]
        return ring_pair(up_block, up_next, z_up, down_block, down_next, z_down, k + hop)

    def along_y(view, low, high, k, hop):
        up_block, down_block = view((y + Y - hop) % Y), view((y + hop) % Y)
        up_next, down_next = view((y + Y - hop - 1) % Y), view((y + hop + 1) % Y)
        if hop == 1:
            up_block, up_next = up_block.at[low], up_next.at[low]
            down_block, down_next = down_block.at[high], down_next.at[high]
        return ring_pair(up_block, up_next, y_up, down_block, down_next, y_down, k + hop)

    def ring_pair(up_block, up_next, up_peer, down_block, down_next, down_peer, k):
        def side(i, peer):
            return lambda block: remote(block, block, w_send.at[k, i], w_recv.at[k, i], peer)

        return (
            Pair(side(0, up_peer), up_block, up_next),
            Pair(side(1, down_peer), down_block, down_next),
        )

    first_rows, last_rows = pl.ds(0, HD // 2), pl.ds(HD // 2, HD // 2)

    def a1(hop):
        return along_y(lambda k: weights_a.at[z, k], first_rows, last_rows, 0, hop)

    def a2(hop):
        return along_z(lambda k: weights_a.at[k], pl.ds(0, 2), pl.ds(2, 2), 2, hop)

    def b1(hop):
        return along_z(lambda k: weights_b.at[k, y], first_rows, last_rows, 6, hop)

    def planes_pair(k, distance):
        return weights_b.at[pl.ds(2 * k, 2), (y + distance) % Y]

    def b2_near(k):
        other = (k + 2) % 4
        return ring_pair(
            planes_pair(k, 0), planes_pair(k, 3), y_up,
            planes_pair(other, 0), planes_pair(other, 1), y_down, 10 + k,
        )

    def b2_far(k):
        return ring_pair(
            planes_pair(k, 3), planes_pair(k, 2), y_up,
            planes_pair(k + 2, 1), planes_pair(k + 2, 2), y_down, 14 + k,
        )

    def start(copies):
        for copy in copies:
            copy.start()

    def arrived(copies):
        for copy in copies:
            copy.wait_recv()

    def pass_on(i):
        arrived(first_leg(i))
        start(second_leg(i))

    loads[0].wait()
    start(q_copies(0))
    loads[2].wait()
    loads[3].wait()
    loads[1].wait()
    for i in range(AHEAD):
        pack(i)
        start(first_leg(i))
        start(direct(i))
        if i == 0:
            start(a1(0))
            start(b1(0))
    lax.fori_loop(0, 16, keep, 0)

    state_o[0] = jnp.zeros((HD, LANES), jnp.float32)
    state_m[0] = jnp.full((1, LANES), LOW, jnp.float32)
    state_l[0] = jnp.zeros((1, LANES), jnp.float32)

    def soften(scores, m_before):
        m = jnp.maximum(m_before, jnp.max(scores, axis=0, keepdims=True))
        expo = jnp.exp2(scores - m)
        return m, jnp.sum(expo, axis=0, keepdims=True), expo.astype(jnp.bfloat16)

    def attend_steps(p, _):
        rows = pl.ds(pl.multiple_of(p * SPAN, SPAN), SPAN)
        mask = mask_ref[p]
        mask = jnp.concatenate([mask] * GROUP, axis=1)
        scores = dot(step_ref[0, rows, :], qs[0][p]) * SCALE
        scores = jnp.where(mask > 0.5, scores, LOW)
        m, l, weights = soften(scores, jnp.full((1, LANES), LOW, jnp.float32))
        step_o[p] = dot(step_ref[1, rows, :], weights, ((0,), (0,)))
        step_m[p] = m
        step_l[p] = l
        return 0

    def attend_tiles(turn):
        queries = qs[ORDER[turn]]

        def one(s, _):
            slot = meta_ref[META_ORDER + turn * 8 + s]
            owner = meta_ref[META_OWNER + turn * 8 + s]
            same = meta_ref[META_SAME + turn * 8 + s]
            scores = dot(pool_ref[slot, 0], queries[owner]) * SCALE
            m_before = jnp.where(same > 0, state_m[s], LOW)
            m, l, weights = soften(scores, m_before)
            alpha = jnp.exp2(m_before - m)
            state_o[s + 1] = state_o[s] * alpha + dot(pool_ref[slot, 1], weights, ((0,), (0,)))
            state_m[s + 1] = m
            state_l[s + 1] = state_l[s] * alpha + l
            return 0

        lax.fori_loop(0, 8, one, 0)

    def sums(hop, p, side):
        out, out_s, inn, inn_s, peer = (
            (up_out, up_out_s, up_in, up_in_s, z_up),
            (down_out, down_out_s, down_in, down_in_s, z_down),
        )[side]
        return (
            remote(out.at[hop, p], inn.at[hop, p], c_send.at[hop, side, p, 0], c_recv.at[hop, side, p, 0], peer),
            remote(out_s.at[hop, p], inn_s.at[hop, p], c_send.at[hop, side, p, 1], c_recv.at[hop, side, p, 1], peer),
        )

    def pass_sums(hop, turn, side):
        out, out_s, inn, inn_s = (
            (up_out, up_out_s, up_in, up_in_s),
            (down_out, down_out_s, down_in, down_in_s),
        )[side]

        def alone(p, _):
            last = meta_ref[META_LAST + turn * 4 + p]
            out[hop, p] = state_o[last].astype(jnp.bfloat16)
            out_s[hop, p, :, 0:LANES] = state_m[last]
            out_s[hop, p, :, LANES:] = state_l[last]
            start(sums(hop, p, side))
            return 0

        def merged(p, _):
            last = meta_ref[META_LAST + turn * 4 + p]
            arrived(sums(hop - 1, p, side))
            m_a, m_b = state_m[last], inn_s[hop - 1, p, :, 0:LANES]
            m = jnp.maximum(m_a, m_b)
            a, b = jnp.exp2(m_a - m), jnp.exp2(m_b - m)
            out[hop, p] = (state_o[last] * a + inn[hop - 1, p].astype(jnp.float32) * b).astype(
                jnp.bfloat16
            )
            out_s[hop, p, :, 0:LANES] = m
            out_s[hop, p, :, LANES:] = state_l[last] * a + inn_s[hop - 1, p, :, LANES:] * b
            start(sums(hop, p, side))
            return 0

        half = HALVES[side]
        if hop == 0:
            lax.fori_loop(*half, alone, 0)
        elif hop == 1 and side == 0:
            lax.fori_loop(0, 2, alone, 0)
            lax.fori_loop(2, 4, merged, 0)
        elif hop == 1:
            lax.fori_loop(0, 2, merged, 0)
            lax.fori_loop(2, 4, alone, 0)
        else:
            lax.fori_loop(0, 4, merged, 0)

    for hop in range(3):
        arrived(q_copies(hop))
        start(q_copies(hop + 1))
        pass_on(hop)
        arrived(b1(hop))
        start(b1(hop + 1))
        if hop == 0:
            arrived(a1(0))
            start(a1(1))
    for i in range(3, AHEAD):
        pass_on(i)
    loads[4].wait()
    loads[5].wait()
    lax.fori_loop(0, PROBLEMS, attend_steps, 0)
    arrived(a1(1))

    legs = {
        0: [(b1, 3, None, 0)],
        6: [(None, 0, a2, 0)],
    }
    for i in range(8):
        rz = ORDER[i]
        if i < chunks:
            join(i)
        ahead = i + AHEAD
        if ahead < chunks:
            pack(ahead)
            start(first_leg(ahead))
            start(direct(ahead))
        if AHEAD <= ahead - 1 < chunks:
            pass_on(ahead - 1)
        if i == 0:
            arrived(q_copies(3))
        if i == B2_TURN:
            for k in range(4):
                start(b2_near(k))
        attend_tiles(i)
        if rz == 4:
            pass_sums(0, i, 0)
            pass_sums(0, i, 1)
        elif rz in (3, 2, 1):
            pass_sums(4 - rz, i, 0)
        elif rz in (5, 6, 7):
            pass_sums(rz - 4, i, 1)
        for before, hop, after, next_hop in legs.get(i, ()):
            if before is not None:
                arrived(before(hop))
            if after is not None:
                start(after(next_hop))
        if i == 6:
            arrived(b2_near(0))
            start(b2_far(0))
    mine = tensor

    def finish(p):
        arrived(sums(3, p, 0))
        arrived(sums(3, p, 1))
        last = meta_ref[META_LAST + 28 + p]
        terms = (
            (state_o[last], state_m[last], state_l[last]),
            (step_o[p], step_m[p], step_l[p]),
            (up_in[3, p].astype(jnp.float32), up_in_s[3, p, :, 0:LANES], up_in_s[3, p, :, LANES:]),
            (down_in[3, p].astype(jnp.float32), down_in_s[3, p, :, 0:LANES], down_in_s[3, p, :, LANES:]),
        )
        m = functools.reduce(jnp.maximum, [t[1] for t in terms])
        factors = [jnp.exp2(t[1] - m) for t in terms]
        total = sum(t[2] * f for t, f in zip(terms, factors))
        result = sum(t[0] * f for t, f in zip(terms, factors)) / total
        for h in range(GROUP):
            block = result[:, h * LIVE : (h + 1) * LIVE]
            heads[mine, p, :, h * HD : (h + 1) * HD] = block.T.astype(jnp.bfloat16)

    left, right, far = (x + X - 1) % X, (x + 1) % X, (x + 2) % X

    def to(k, p, owner, peer):
        view = heads.at[owner, p]
        return remote(view, view, x_send.at[k, p], x_recv.at[k, p], peer)

    def own_heads(p):
        return to(0, p, mine, x_up), to(1, p, mine, x_down), to(2, p, mine, mate)

    def next_heads(p):
        onward = to(3, p, left * 2 + core, x_up) if p < 2 else to(3, p, right * 2 + core, x_down)
        return onward, to(4, p, left * 2 + core, mate), to(5, p, right * 2 + core, mate)

    def near_heads(p):
        return to(0, p, left * 2 + core, x_up), to(1, p, right * 2 + core, x_down)

    def far_heads(p):
        return (to(3, p, far * 2 + core, x_up if p < 2 else x_down),)

    def last_heads(p):
        return (to(6, p, far * 2 + core, mate),)

    def mate_heads(p):
        other = 1 - core
        return (
            to(2, p, x * 2 + other, mate),
            to(4, p, left * 2 + other, mate),
            to(5, p, right * 2 + other, mate),
            to(6, p, far * 2 + other, mate),
        )

    for p in range(PROBLEMS):
        finish(p)
        start(own_heads(p))
        if p > 0:
            arrived(near_heads(p - 1))
            start(next_heads(p - 1))
        if p == 2:
            arrived(a2(0))
            start(a2(1))
            arrived(b2_near(1))
            start(b2_far(1))
    arrived(near_heads(3))
    start(next_heads(3))
    arrived(a2(1))
    start(a2(2))
    for p in range(PROBLEMS):
        arrived(far_heads(p))
        start(last_heads(p))
    arrived(a2(2))
    start(a2(3))
    for p in range(PROBLEMS):
        arrived(mate_heads(p))

    def product(weights, t, columns):
        block = weights[t, :, :, columns].reshape(LANES, 256)
        return dot(heads[t].reshape(PROBLEMS * LIVE, LANES), block)

    def part_b(planes, more):
        def block(c, _):
            columns = pl.ds(pl.multiple_of(c * 256, 256), 256)
            total = sum(product(weights_b, t, columns) for t in planes)
            into = pl.ds(pl.multiple_of(PART_A + c * 256, 256), 256)
            if more:
                total_b[:, columns] = total
            else:
                out_ref[:, into] = (total_b[:, columns] + total).astype(jnp.bfloat16)
            return 0

        lax.fori_loop(0, PART_B // 256, block, 0)

    for k in range(2, 4):
        arrived(b2_near(k))
    arrived(b2_far(0))
    part_b((0, 1, 4, 5), True)
    arrived(a2(3))
    total_a = sum(product(weights_a, t, pl.ds(0, PART_A)) for t in range(8))
    out_ref[:, 0:PART_A] = total_a.astype(jnp.bfloat16)
    arrived(b2_far(1))
    part_b((2, 3, 6, 7), False)

    for p in range(PROBLEMS):
        for copy in own_heads(p) + next_heads(p) + last_heads(p):
            copy.wait_send()
    for hop in range(4):
        for copy in q_copies(hop) + a2(hop) + b1(hop):
            copy.wait_send()
        for side in range(2):
            for p in range(*HALVES[side]) if hop == 0 else range(PROBLEMS):
                for copy in sums(hop, p, side):
                    copy.wait_send()
    for hop in range(2):
        for copy in a1(hop) + b2_far(hop):
            copy.wait_send()
    for k in range(4):
        for copy in b2_near(k):
            copy.wait_send()
    for i in range(chunks):
        for copy in direct(i) + first_leg(i) + second_leg(i):
            copy.wait_send()


def expand_kernel(compact_ref, expand_ref, out_ref):
    for p in range(PROBLEMS):
        out_ref[p * SPAN : (p + 1) * SPAN, :] = dot(
            expand_ref[p], compact_ref[p * LIVE : (p + 1) * LIVE, :]
        ).astype(jnp.bfloat16)


def per_device(queries, step_kv, tile_kv, tile_slot, step_lengths, parents, out_weight):
    bf16, f32, i32 = jnp.bfloat16, jnp.float32, jnp.int32
    smem = pl.BlockSpec(memory_space=pltpu.SMEM)
    vmem = pl.BlockSpec(memory_space=pltpu.VMEM)
    hbm = pl.BlockSpec(memory_space=pl.ANY)
    columns = out_weight.shape[1]

    qt, mask, expand, meta, choice = pl.pallas_call(
        prep_kernel,
        out_shape=(
            jax.ShapeDtypeStruct((PROBLEMS, HD, LANES), bf16),
            jax.ShapeDtypeStruct((PROBLEMS, SPAN, LIVE), f32),
            jax.ShapeDtypeStruct((PROBLEMS, SPAN, LIVE), bf16),
            jax.ShapeDtypeStruct((512,), i32),
            jax.ShapeDtypeStruct((1,), i32),
        ),
        in_specs=[hbm] * 5,
        out_specs=(vmem, vmem, vmem, smem, smem),
        scratch_shapes=[
            pltpu.SMEM((1024,), i32),
            pltpu.VMEM((8, 128), i32),
            pltpu.SMEM((STEPS, 128), i32),
            pltpu.SMEM((STEPS, 128), i32),
            pltpu.VMEM(queries.shape, bf16),
            pltpu.SMEM((32,), i32),
            pltpu.SMEM((32,), i32),
            pltpu.SMEM((8,), i32),
            pltpu.SMEM((64,), i32),
            pltpu.SMEM((64,), i32),
            pltpu.SMEM((64,), i32),
            pltpu.SemaphoreType.DMA((5,)),
        ],
        compiler_params=pltpu.CompilerParams(vmem_limit_bytes=VMEM),
        cost_estimate=pl.CostEstimate(flops=100_000_000, bytes_accessed=4_000_000, transcendentals=0),
        name="prep",
    )(tile_slot, tile_slot.reshape(8, 128), step_lengths.T, parents.T, queries)

    planes = lambda number, capacity: pl.pallas_call(
        functools.partial(plane_kernel, capacity),
        out_shape=jax.ShapeDtypeStruct((PROBLEMS * LIVE, columns), bf16),
        in_specs=[smem] + [hbm] * 5,
        out_specs=vmem,
        scratch_shapes=[pltpu.VMEM((PROBLEMS, HD, LANES), bf16)] * 8
        + [
            pltpu.VMEM((PROBLEMS, SPAN, LIVE), f32),
            pltpu.VMEM(step_kv.shape, bf16),
            pltpu.VMEM((2, 32, TILE, HD), bf16),
            pltpu.VMEM((3, capacity, 2, TILE, HD), bf16),
            pltpu.VMEM((3, capacity, 2, TILE, HD), bf16),
            pltpu.VMEM((64, 2, TILE, HD), bf16),
            pltpu.VMEM((Z, Y, HD, PART_A), bf16),
            pltpu.VMEM((Z, Y, HD, PART_B), bf16),
            pltpu.VMEM((8, PROBLEMS, LIVE, LANES), bf16),
            pltpu.VMEM((2, capacity, TILE, HD), bf16),
            pltpu.VMEM((9, HD, LANES), f32),
            pltpu.VMEM((9, 1, LANES), f32),
            pltpu.VMEM((9, 1, LANES), f32),
            pltpu.VMEM((PROBLEMS, HD, LANES), f32),
            pltpu.VMEM((PROBLEMS, 1, LANES), f32),
            pltpu.VMEM((PROBLEMS, 1, LANES), f32),
        ]
        + [
            pltpu.VMEM((4, PROBLEMS, HD, LANES), bf16),
            pltpu.VMEM((4, PROBLEMS, 1, 2 * LANES), f32),
        ]
        * 4
        + [
            pltpu.VMEM((PROBLEMS * LIVE, PART_B), f32),
            pltpu.SemaphoreType.DMA((8,)),
            pltpu.SemaphoreType.DMA((8, 6)),
            pltpu.SemaphoreType.DMA((8, 6)),
            pltpu.SemaphoreType.DMA((4, 2)),
            pltpu.SemaphoreType.DMA((4, 2)),
            pltpu.SemaphoreType.DMA((4, 2, 4, 2)),
            pltpu.SemaphoreType.DMA((4, 2, 4, 2)),
            pltpu.SemaphoreType.DMA((7, 4)),
            pltpu.SemaphoreType.DMA((7, 4)),
            pltpu.SemaphoreType.DMA((16, 2)),
            pltpu.SemaphoreType.DMA((16, 2)),
        ],
        compiler_params=pltpu.CompilerParams(
            collective_id=number, has_side_effects=True, vmem_limit_bytes=VMEM
        ),
        cost_estimate=pl.CostEstimate(
            flops=60_000_000_000, bytes_accessed=300_000_000, transcendentals=10_000_000
        ),
        name="planes",
    )
    compact = lax.switch(
        choice[0],
        [planes(number, capacity) for number, capacity in enumerate(CAPACITIES)],
        meta, qt, mask, step_kv, tile_kv.reshape(2, 32, TILE, HD), out_weight,
    )

    block = 512
    return pl.pallas_call(
        expand_kernel,
        out_shape=jax.ShapeDtypeStruct((PROBLEMS * SPAN, columns), bf16),
        grid=(columns // block,),
        in_specs=[
            pl.BlockSpec((PROBLEMS * LIVE, block), lambda i: (0, i)),
            pl.BlockSpec((PROBLEMS, SPAN, LIVE), lambda i: (0, 0, 0)),
        ],
        out_specs=pl.BlockSpec((PROBLEMS * SPAN, block), lambda i: (0, i)),
        compiler_params=pltpu.CompilerParams(vmem_limit_bytes=VMEM),
        cost_estimate=pl.CostEstimate(
            flops=200_000_000, bytes_accessed=3_000_000, transcendentals=0
        ),
        name="expand",
    )(compact, expand)


def solution(mesh):
    return jax.shard_map(
        per_device,
        mesh=mesh,
        in_specs=(
            P("dp", "tensor"),
            P(None, "dp", "tensor"),
            P(None, "dp", "tensor"),
            P(),
            P(),
            P(),
            P("dp", "tensor"),
        ),
        out_specs=P("dp", "tensor"),
        check_vma=False,
    )
```

time: 182 us -> 161 us (0.88); the launches traced: 179 us -> 161 us
  Pallas kernels: 179 us -> 159 us
    pallas_call x1, Pallas kernels: 168 us -> 146 us  [per_device(): lax.switch(choice[0], [planes(number, capacity) for number, capacity in e...]
    pallas_call x1, Pallas kernels: 7.87 us -> 10.6 us  [per_device(): pl.pallas_call(prep_kernel, out_shape=(jax.ShapeDtypeStruct((PROBLEMS, HD...]
where the time goes in v3:
time: 161 us
  Pallas kernels  159 us (99%)
    pallas_call x1, Pallas kernels, per_device(): lax.switch(choice[0], [planes(number, capacity) for number, capacity in e...  146 us
    pallas_call x1, Pallas kernels, per_device(): pl.pallas_call(prep_kernel, out_shape=(jax.ShapeDtypeStruct((PROBLEMS, HD...  10.6 us

profile of v3, /device:TPU:6, one launch (start us, length us, event | category | flops | bytes accessed | tf_op | source)
XLA Modules:
  0.0 160.9 jit_solution(1366539512600229899)
XLA Ops:
  0.0 10.6 %prep.1 = (bf16[4,128,512]{2,1,0:T(8,128)(2,1)S(1)}, f32[4,192,128]{2,1,0:T(8,128)S(1)}, bf16[4,192,128]{2,1,0:T(8,128)(2,1)}, s32[512]{0:T(512)S(1)}, s32[1]{0:T(128)}) custom-call(s32[1024]{0:T(1024)} %slot_hbm.1, s32[8,128]{1,0:T(8,128)} %bitcast.5, s32[8,128]{1,0:T(8,128)} %bitcast.6, s32[8,128]{1,0:T(8,128)} %bitcast.7, bf16[768,512]{1,0:T(8,128)(2,1)} %query_hbm.1), custom_call_target="tpu_custom_call" | custom-call | flops 100000000 | bytes 4000000 | tf_op jit(solution)/shard_map/prep/pallas_call | solution.py:694
  11.2 147.0 %conditional.1 = (bf16[512,1024]{1,0:T(8,128)(2,1)S(1)}) conditional(s32[]{:T(128)} %bitcast.3, (s32[512]{0:T(512)S(1)}, bf16[4,128,512]{2,1,0:T(8,128)(2,1)S(1)}, f32[4,192,128]{2,1,0:T(8,128)S(1)}, bf16[2,768,128]{2,1,0:T(8,128)(2,1)}, bf16[2,32,256,128]{3,2,1,0:T(8,128)(2,1)}, /*index=5*/bf16[128,1024]{1,0:T(8,128)(2,1)}) %tuple.18, ...), branch_computations={%region_0.0_spmd, %region_1.0_spmd, %region_2.0_spmd} | conditional | flops 60000002048 | bytes 300000000 | solution.py:775
  11.5 146.3 %planes.4 = bf16[512,1024]{1,0:T(8,128)(2,1)S(1)} custom-call(s32[512]{0:T(512)S(1)} %get-tuple-element.51.meta_ref, bf16[4,128,512]{2,1,0:T(8,128)(2,1)S(1)} %get-tuple-element.52.qt_hbm, f32[4,192,128]{2,1,0:T(8,128)S(1)} %get-tuple-element.53.mask_hbm, bf16[2,768,128]{2,1,0:T(8,128)(2,1)} %get-tuple-element.54.step_hbm, ...), custom_call_target="tpu_custom_call" | custom-call | flops 60000002048 | bytes 300000000 | tf_op jit(solution)/shard_map/cond/branch_1_fun/planes/pallas_call | solution.py:775
  158.3 2.6 %expand.1 = bf16[768,1024]{1,0:T(8,128)(2,1)} custom-call(bf16[512,1024]{1,0:T(8,128)(2,1)S(1)} %get-tuple-element.73.compact_ref, bf16[4,192,128]{2,1,0:T(8,128)(2,1)} %get-tuple-element.72.expand_ref), custom_call_target="tpu_custom_call" | custom-call | flops 200000000 | bytes 3000000 | tf_op jit(solution)/shard_map/expand/pallas_call | solution.py:782

commit v4 on v3

--- a/solution.py
+++ b/solution.py
@@ -91,7 +91,7 @@
         meta_ref[META_SOURCE + i] = 0
         return 0
 
-    lax.fori_loop(0, 64, clear_slots, 0)
+    lax.fori_loop(0, 64, clear_slots, 0, unroll=8)
     for i, rz in enumerate(ORDER):
         rank[rz] = i
     loads[0].wait()
@@ -105,7 +105,7 @@
         given[r * 16 + turn * 2 + j] = t
         return 0
 
-    lax.fori_loop(0, 32, place, 0)
+    lax.fori_loop(0, 32, place, 0, unroll=4)
 
     def arrive(q, _):
         s = slot_ref[z * 128 + q]
@@ -121,7 +121,7 @@
 
         return 0
 
-    lax.fori_loop(0, 128, arrive, 0)
+    lax.fori_loop(0, 128, arrive, 0, unroll=8)
 
     def close(i, carry):
         sent, got = carry
@@ -137,7 +137,7 @@
         place_of[i] = base + got
         return sent + give.astype(jnp.int32), got + take.astype(jnp.int32)
 
-    lax.fori_loop(0, 64, close, (0, 0))
+    lax.fori_loop(0, 64, close, (0, 0), unroll=8)
 
     def arrange(i, n):
         turn, p = i // 4, i % 4
@@ -158,7 +158,7 @@
             hit = match.astype(jnp.int32)
             return n + hit, jnp.maximum(seen, hit)
 
-        n, _ = lax.fori_loop(0, 8, scan, (n, 0))
+        n, _ = lax.fori_loop(0, 8, scan, (n, 0), unroll=True)
         return n
 
     lax.fori_loop(0, 32, arrange, 0)
@@ -451,7 +451,7 @@
             state_l[s + 1] = state_l[s] * alpha + l
             return 0
 
-        lax.fori_loop(0, 8, one, 0)
+        lax.fori_loop(0, 8, one, 0, unroll=2)
 
     def sums(hop, p, side):
         out, out_s, inn, inn_s, peer = (

time: 161 us -> 154 us (0.957)
  Pallas kernels: 159 us -> 153 us
    pallas_call x1, Pallas kernels: 10.6 us -> 6.16 us  [per_device(): pl.pallas_call(prep_kernel, out_shape=(jax.ShapeDtypeStruct((PROBLEMS, HD...]
    pallas_call x1, Pallas kernels: 146 us -> 144 us  [per_device(): lax.switch(choice[0], [planes(number, capacity) for number, capacity in e...]
where the time goes in v4:
time: 154 us; the launch traced here: 153 us
  Pallas kernels  153 us (99%)
    pallas_call x1, Pallas kernels, per_device(): lax.switch(choice[0], [planes(number, capacity) for number, capacity in e...  144 us
    pallas_call x1, Pallas kernels, per_device(): pl.pallas_call(prep_kernel, out_shape=(jax.ShapeDtypeStruct((PROBLEMS, HD...  6.16 us

profile of v4, /device:TPU:6, one launch (start us, length us, event | category | flops | bytes accessed | tf_op | source)
XLA Modules:
  0.0 153.5 jit_solution(12631481821404824107)
XLA Ops:
  0.0 6.2 %prep.1 = (bf16[4,128,512]{2,1,0:T(8,128)(2,1)S(1)}, f32[4,192,128]{2,1,0:T(8,128)S(1)}, bf16[4,192,128]{2,1,0:T(8,128)(2,1)}, s32[512]{0:T(512)S(1)}, s32[1]{0:T(128)}) custom-call(s32[1024]{0:T(1024)} %slot_hbm.1, s32[8,128]{1,0:T(8,128)} %bitcast.5, s32[8,128]{1,0:T(8,128)} %bitcast.6, s32[8,128]{1,0:T(8,128)} %bitcast.7, bf16[768,512]{1,0:T(8,128)(2,1)} %query_hbm.1), custom_call_target="tpu_custom_call" | custom-call | flops 100000000 | bytes 4000000 | tf_op jit(solution)/shard_map/prep/pallas_call | solution.py:694
  6.8 144.1 %conditional.1 = (bf16[512,1024]{1,0:T(8,128)(2,1)S(1)}) conditional(s32[]{:T(128)} %bitcast.3, (s32[512]{0:T(512)S(1)}, bf16[4,128,512]{2,1,0:T(8,128)(2,1)S(1)}, f32[4,192,128]{2,1,0:T(8,128)S(1)}, bf16[2,768,128]{2,1,0:T(8,128)(2,1)}, bf16[2,32,256,128]{3,2,1,0:T(8,128)(2,1)}, /*index=5*/bf16[128,1024]{1,0:T(8,128)(2,1)}) %tuple.18, ...), branch_computations={%region_0.0_spmd, %region_1.0_spmd, %region_2.0_spmd} | conditional | flops 60000002048 | bytes 300000000 | solution.py:775
  6.8 143.8 %planes.3 = bf16[512,1024]{1,0:T(8,128)(2,1)S(1)} custom-call(s32[512]{0:T(512)S(1)} %get-tuple-element.44.meta_ref, bf16[4,128,512]{2,1,0:T(8,128)(2,1)S(1)} %get-tuple-element.46.qt_hbm, f32[4,192,128]{2,1,0:T(8,128)S(1)} %get-tuple-element.47.mask_hbm, bf16[2,768,128]{2,1,0:T(8,128)(2,1)} %get-tuple-element.48.step_hbm, ...), custom_call_target="tpu_custom_call" | custom-call | flops 60000002048 | bytes 300000000 | tf_op jit(solution)/shard_map/cond/branch_0_fun/planes/pallas_call | solution.py:775
  150.9 2.6 %expand.1 = bf16[768,1024]{1,0:T(8,128)(2,1)} custom-call(bf16[512,1024]{1,0:T(8,128)(2,1)S(1)} %get-tuple-element.73.compact_ref, bf16[4,192,128]{2,1,0:T(8,128)(2,1)} %get-tuple-element.72.expand_ref), custom_call_target="tpu_custom_call" | custom-call | flops 200000000 | bytes 3000000 | tf_op jit(solution)/shard_map/expand/pallas_call | solution.py:782

commit v5 on v4

--- a/solution.py
+++ b/solution.py
@@ -29,7 +29,7 @@
 PART_A = 256
 PART_B = 768
 HALVES = ((2, 4), (0, 2))
-AHEAD = 4
+AHEAD = 5
 B2_TURN = 3
 
 META_ORDER = 0

time: 154 us -> 159 us (1.032)
  Pallas kernels: 153 us -> 158 us
    pallas_call x1, Pallas kernels: 144 us -> 149 us  [per_device(): lax.switch(choice[0], [planes(number, capacity) for number, capacity in e...]
where the time goes in v5:
time: 159 us
  Pallas kernels  158 us (99%)
    pallas_call x1, Pallas kernels, per_device(): lax.switch(choice[0], [planes(number, capacity) for number, capacity in e...  149 us
    pallas_call x1, Pallas kernels, per_device(): pl.pallas_call(prep_kernel, out_shape=(jax.ShapeDtypeStruct((PROBLEMS, HD...  6.16 us

profile of v5, /device:TPU:6, one launch (start us, length us, event | category | flops | bytes accessed | tf_op | source)
XLA Modules:
  0.0 158.6 jit_solution(15898922777893219002)
XLA Ops:
  0.0 6.2 %prep.1 = (bf16[4,128,512]{2,1,0:T(8,128)(2,1)S(1)}, f32[4,192,128]{2,1,0:T(8,128)S(1)}, bf16[4,192,128]{2,1,0:T(8,128)(2,1)}, s32[512]{0:T(512)S(1)}, s32[1]{0:T(128)}) custom-call(s32[1024]{0:T(1024)} %slot_hbm.1, s32[8,128]{1,0:T(8,128)} %bitcast.5, s32[8,128]{1,0:T(8,128)} %bitcast.6, s32[8,128]{1,0:T(8,128)} %bitcast.7, bf16[768,512]{1,0:T(8,128)(2,1)} %query_hbm.1), custom_call_target="tpu_custom_call" | custom-call | flops 100000000 | bytes 4000000 | tf_op jit(solution)/shard_map/prep/pallas_call | solution.py:694
  6.8 149.2 %conditional.1 = (bf16[512,1024]{1,0:T(8,128)(2,1)S(1)}) conditional(s32[]{:T(128)} %bitcast.3, (s32[512]{0:T(512)S(1)}, bf16[4,128,512]{2,1,0:T(8,128)(2,1)S(1)}, f32[4,192,128]{2,1,0:T(8,128)S(1)}, bf16[2,768,128]{2,1,0:T(8,128)(2,1)}, bf16[2,32,256,128]{3,2,1,0:T(8,128)(2,1)}, /*index=5*/bf16[128,1024]{1,0:T(8,128)(2,1)}) %tuple.18, ...), branch_computations={%region_0.0_spmd, %region_1.0_spmd, %region_2.0_spmd} | conditional | flops 60000002048 | bytes 300000000 | solution.py:775
  6.8 148.9 %planes.3 = bf16[512,1024]{1,0:T(8,128)(2,1)S(1)} custom-call(s32[512]{0:T(512)S(1)} %get-tuple-element.44.meta_ref, bf16[4,128,512]{2,1,0:T(8,128)(2,1)S(1)} %get-tuple-element.46.qt_hbm, f32[4,192,128]{2,1,0:T(8,128)S(1)} %get-tuple-element.47.mask_hbm, bf16[2,768,128]{2,1,0:T(8,128)(2,1)} %get-tuple-element.48.step_hbm, ...), custom_call_target="tpu_custom_call" | custom-call | flops 60000002048 | bytes 300000000 | tf_op jit(solution)/shard_map/cond/branch_0_fun/planes/pallas_call | solution.py:775
  156.0 2.6 %expand.1 = bf16[768,1024]{1,0:T(8,128)(2,1)} custom-call(bf16[512,1024]{1,0:T(8,128)(2,1)S(1)} %get-tuple-element.73.compact_ref, bf16[4,192,128]{2,1,0:T(8,128)(2,1)} %get-tuple-element.72.expand_ref), custom_call_target="tpu_custom_call" | custom-call | flops 200000000 | bytes 3000000 | tf_op jit(solution)/shard_map/expand/pallas_call | solution.py:782
